TPU v7x, 512 devices: a whole 4x8x8 slice. The times are simulated.
512 devices in a mesh: roll: 64 (over x, z, core), side: 8 (over y).
Axes of the slice: x: 4, y: 8, z: 8, core: 2. Of those that a mesh axis runs over, the one named last changes fastest.
Arguments:
- pressure: float32 [8192, 2048], P('roll', 'side'), may hold values from -6 to 6
- source: float32 [8192, 2048], P('roll', 'side'), may hold values from -6 to 6
- side_coupling: float32 [8192, 2048], P('roll', 'side'), may hold values from 0.4 to 0.8
- block_inverse: float32 [8192, 1024], P('roll', 'side'), may hold values from -1 to 1
- lower_coupling: float32 [64, 2048], P('roll', 'side'), may hold values from 0.5 to 30
- cavity_mask: int32 [64, 2048], P('roll', 'side'), may hold values 0 or 1
- rough_code: int32 [8192, 2048], P('roll', 'side'), may hold values from 0 to 15
- film_offset: float32 [1], replicated, may hold values from 0.5 to 1.5
Outputs:
- new_pressure: float32 [8192, 2048], P('roll', 'side')
- film: float32 [8192, 2048], P('roll', 'side')
All inputs are finite; a program needn't handle non-finite values. No bound on the sum of `cavity_mask` on one device may be relied on, other than what follows from the above.
Results may differ from a plain program's by a relative error of at most 0.00018.
Values sent between devices are 32-bit elements; how exact they have to be, the bound alone decides.
A program may use at most 64 MiB of HBM per device.

v0:
```python
import math

import jax
import jax.numpy as jnp
from jax import lax
from jax.sharding import PartitionSpec as P

SWEEPS = 4


HIGHEST = lax.Precision.HIGHEST
TWO_PI = 2.0 * math.pi
ROUGH_STEP = 0.05


def padded_2(cells, sides, width):
    for axis, dim in sides:
        count = lax.axis_size(axis)
        ends = count - 1
        head = lax.slice_in_dim(cells, 0, width, axis=dim)
        tail = lax.slice_in_dim(cells, cells.shape[dim] - width, cells.shape[dim], axis=dim)
        cells = jnp.concatenate(
            [
                lax.ppermute(tail, axis, [(i, (i + 1) % count) for i in range(ends)]),
                cells,
                lax.ppermute(head, axis, [((i + 1) % count, i) for i in range(ends)]),
            ],
            axis=dim,
        )
    return cells


def entering(part, axis, combine, identity):
    place = lax.axis_index(axis)
    gathered = jax.tree.map(lambda a: lax.all_gather(a, axis), part)
    state = jax.tree.map(lambda a, e: jnp.zeros_like(a) + jnp.asarray(e, a.dtype), part, identity)

    def one(turn, state):
        return combine(
            state, jax.tree.map(lambda a: lax.dynamic_index_in_dim(a, turn, 0, False), gathered)
        )

    return lax.fori_loop(0, place, one, state)


def counting(length):
    return jnp.arange(length, dtype=jnp.int32)


def phase_pair(first_ints, second_ints, length, sign_value):
    angles = (first_ints * second_ints % length).astype(jnp.float32) * (TWO_PI / length)
    return (jnp.cos(angles), sign_value * jnp.sin(angles))


def complex_product(formula, left_re, left_im, right_re, right_im):
    real_part = jnp.einsum(formula, left_re, right_re, precision=HIGHEST) - jnp.einsum(
        formula, left_im, right_im, precision=HIGHEST
    )
    imag_part = jnp.einsum(formula, left_re, right_im, precision=HIGHEST) + jnp.einsum(
        formula, left_im, right_re, precision=HIGHEST
    )
    return (real_part, imag_part)


def rotate(values_re, values_im, turn_re, turn_im):
    return (values_re * turn_re - values_im * turn_im, values_re * turn_im + values_im * turn_re)


def compose_maps(earlier_map, later_map):
    return (earlier_map[0] * later_map[0], later_map[0] * earlier_map[1] + later_map[1])


def spectrum_position(col_count):
    position = counting(col_count)
    return position


def column_forward(values_re, values_im):
    col_count = values_re.shape[-1]
    position = counting(col_count)
    table_re, table_im = phase_pair(position[:, None], position[None, :], col_count, -1.0)
    return complex_product("xvc,cw->xvw", values_re, values_im, table_re, table_im)


def column_inverse(values_re, values_im):
    col_count = values_re.shape[-1]
    position = counting(col_count)
    table_re, table_im = phase_pair(position[:, None], position[None, :], col_count, 1.0)
    return complex_product("xvw,wc->xvc", values_re, values_im, table_re, table_im)


def per_device(
    pressure,
    source,
    side_coupling,
    block_inverse,
    lower_coupling,
    cavity_mask,
    rough_code,
    film_offset,
):
    row_count, col_count = pressure.shape
    roll_count = lax.axis_size("roll")
    side_count = lax.axis_size("side")
    roll_place = lax.axis_index("roll")
    side_place = lax.axis_index("side")
    first_column = block_inverse[:, 0:1]
    gain_row = block_inverse[row_count - 1, 0] * lower_coupling[0]
    mask_on = cavity_mask == 1
    identity = (jnp.ones_like(gain_row), jnp.zeros_like(gain_row))
    pressure_now = pressure
    for sweep_step in range(SWEEPS):
        padded = padded_2(pressure_now, (("side", 1),), 1)
        right_side = source + side_coupling * (padded[:, :-2] + padded[:, 2:])
        line_local = jnp.dot(
            block_inverse, right_side, precision=HIGHEST, preferred_element_type=jnp.float32
        )
        prefix = entering((gain_row, line_local[row_count - 1]), "roll", compose_maps, identity)
        solved = line_local + first_column * (lower_coupling * prefix[1][None, :])
        pressure_now = jnp.where(mask_on, jnp.maximum(solved, 0.0), solved)
    double_roll = 2 * roll_count
    fft_rows = row_count * double_roll
    side_freq = 2 * side_count
    fft_cols = side_freq * col_count
    row_index = counting(row_count)
    slot_values = 2 * roll_place + counting(2)
    pieces = lax.all_to_all(pressure_now[None], "roll", split_axis=1, concat_axis=0, tiled=True)
    source_index = counting(pieces.shape[0])
    rows_freq_index = counting(double_roll)
    table_re, table_im = phase_pair(
        rows_freq_index[:, None], source_index[None, :], double_roll, -1.0
    )
    out_re = jnp.einsum("ur,rtk->utk", table_re, pieces, precision=HIGHEST)
    out_im = jnp.einsum("ur,rtk->utk", table_im, pieces, precision=HIGHEST)
    pieces = (
        lax.all_to_all(out_re, "roll", split_axis=0, concat_axis=1, tiled=True),
        lax.all_to_all(out_im, "roll", split_axis=0, concat_axis=1, tiled=True),
    )
    slot_re = pieces[0]
    slot_im = pieces[1]
    turn_re, turn_im = phase_pair(slot_values[:, None], row_index[None, :], fft_rows, -1.0)
    slot_re, slot_im = rotate(slot_re, slot_im, turn_re[:, :, None], turn_im[:, :, None])
    table_re, table_im = phase_pair(row_index[:, None], row_index[None, :], row_count, -1.0)
    spec_re, spec_im = complex_product("ut,xtk->xuk", table_re, table_im, slot_re, slot_im)
    group_size = 2 * row_count // side_count
    freq_index = counting(side_freq)
    side_index = counting(side_count)
    column_index = counting(col_count)
    block_shape = (side_count, group_size, 1, col_count)
    pieces = (
        lax.all_to_all(
            spec_re.reshape(block_shape), "side", split_axis=0, concat_axis=2, tiled=True
        ),
        lax.all_to_all(
            spec_im.reshape(block_shape), "side", split_axis=0, concat_axis=2, tiled=True
        ),
    )
    part_re = pieces[0][0]
    part_im = pieces[1][0]
    table_re, table_im = phase_pair(freq_index[:, None], side_index[None, :], side_freq, -1.0)
    mixed_re, mixed_im = complex_product("vs,ksc->kvc", table_re, table_im, part_re, part_im)
    turn_re, turn_im = phase_pair(freq_index[:, None], column_index[None, :], fft_cols, -1.0)
    mixed_re, mixed_im = rotate(mixed_re, mixed_im, turn_re, turn_im)
    wave_re, wave_im = column_forward(mixed_re, mixed_im)
    item_index = side_place * group_size + counting(group_size)
    slot_index = item_index // row_count
    lane_index = item_index % row_count
    row_freq = jnp.where(slot_index == 0, slot_values[0], slot_values[1]) + double_roll * lane_index
    col_freq = freq_index[:, None] + side_freq * spectrum_position(col_count)[None, :]
    row_wave = jnp.minimum(row_freq, fft_rows - row_freq).astype(jnp.float32) / fft_rows
    col_wave = jnp.minimum(col_freq, fft_cols - col_freq).astype(jnp.float32) / fft_cols
    kernel_reach = min(fft_rows, fft_cols) / 16.0
    radius = jnp.sqrt(
        row_wave[:, None, None] * row_wave[:, None, None] + col_wave[None] * col_wave[None]
    )
    kernel = (
        0.4 * kernel_reach / (float(fft_rows) * float(fft_cols)) / (1.0 + kernel_reach * radius)
    )
    wave_re = wave_re * kernel
    wave_im = wave_im * kernel
    back_re, back_im = column_inverse(wave_re, wave_im)
    turn_re, turn_im = phase_pair(freq_index[:, None], column_index[None, :], fft_cols, 1.0)
    back_re, back_im = rotate(back_re, back_im, turn_re, turn_im)
    table_re, table_im = phase_pair(side_index[:, None], freq_index[None, :], side_freq, 1.0)
    near_re, near_im = complex_product("sv,kvc->ksc", table_re, table_im, back_re, back_im)
    home_re, home_im = (
        lax.all_to_all(near_re[None], "side", split_axis=2, concat_axis=0, tiled=True),
        lax.all_to_all(near_im[None], "side", split_axis=2, concat_axis=0, tiled=True),
    )
    home_re = home_re.reshape(2, row_count, col_count)
    home_im = home_im.reshape(2, row_count, col_count)
    table_re, table_im = phase_pair(row_index[:, None], row_index[None, :], row_count, 1.0)
    line_re, line_im = complex_product("tu,xuc->xtc", table_re, table_im, home_re, home_im)
    turn_re, turn_im = phase_pair(slot_values[:, None], row_index[None, :], fft_rows, 1.0)
    line_re, line_im = rotate(line_re, line_im, turn_re[:, :, None], turn_im[:, :, None])
    place_index = counting(roll_count)
    pieces = (
        lax.all_to_all(line_re, "roll", split_axis=1, concat_axis=0, tiled=True),
        lax.all_to_all(line_im, "roll", split_axis=1, concat_axis=0, tiled=True),
    )
    slot_freq = counting(double_roll)
    cos_table, sin_table = phase_pair(place_index[:, None], slot_freq[None, :], double_roll, 1.0)
    partial_value = jnp.einsum("ru,utk->rtk", cos_table, pieces[0], precision=HIGHEST) - jnp.einsum(
        "ru,utk->rtk", sin_table, pieces[1], precision=HIGHEST
    )
    settled = lax.all_to_all(partial_value, "roll", split_axis=0, concat_axis=1, tiled=True)
    deflection = settled[0]
    row_pos = (roll_place * row_count + row_index).astype(jnp.float32)
    col_pos = (side_place * col_count + column_index).astype(jnp.float32)
    across = 4.0 * (row_pos + 0.5) / (row_count * roll_count) - 2.5
    transverse = 4.0 * (col_pos + 0.5) / (col_count * side_count) - 2.0
    film_height = (
        film_offset[0]
        + 0.5 * across[:, None] * across[:, None]
        + 0.5 * transverse[None, :] * transverse[None, :]
        + deflection
        - ROUGH_STEP * rough_code.astype(jnp.float32)
    )
    return (pressure_now, film_height)


def solution(mesh):
    return jax.shard_map(
        per_device,
        mesh=mesh,
        in_specs=(
            P("roll", "side"),
            P("roll", "side"),
            P("roll", "side"),
            P("roll", "side"),
            P("roll", "side"),
            P("roll", "side"),
            P("roll", "side"),
            P(),
        ),
        out_specs=(P("roll", "side"), P("roll", "side")),
        check_vma=False,
    )
```

profile of v0, /device:TPU:1, one launch (start us, length us, event | category | flops | bytes accessed | tf_op | source)
XLA Modules:
  0.0 474.9 jit_solution(8624491619052037656)
XLA Ops:
  1.6 4.0 collective-permute-start
  8.3 50.6 %all-gather = f32[64,1,256]{2,1,0:T(1,128)S(1)} all-gather(f32[1,1,256]{2,1,0:T(1,128)S(1)} %multiply_bitcast_fusion), channel_id=1, replica_groups=mesh['roll'=64,'side'=8] {'roll'}, dimensions={0}, use_global_device_ids=true | all-gather | bytes 66560 | tf_op jit(solution)/shard_map/all_gather | solution.py:35
  59.7 42.9 %all-gather.1 = f32[64,1,256]{2,1,0:T(1,128)S(1)} all-gather(f32[1,1,256]{2,1,0:T(1,128)S(1)} %bitcast.251), channel_id=1, replica_groups=mesh['roll'=64,'side'=8] {'roll'}, dimensions={0}, use_global_device_ids=true | all-gather | bytes 66560 | tf_op jit(solution)/shard_map/all_gather | solution.py:35
  102.8 4.3 collective-permute-start.2
  108.6 2.8 collective-permute-done.3
  111.9 45.4 %all-gather.2 = f32[64,1,256]{2,1,0:T(1,128)S(1)} all-gather(f32[1,1,256]{2,1,0:T(1,128)S(1)} %bitcast.252), channel_id=1, replica_groups=mesh['roll'=64,'side'=8] {'roll'}, dimensions={0}, use_global_device_ids=true | all-gather | bytes 66560 | tf_op jit(solution)/shard_map/all_gather | solution.py:35
  157.5 3.6 collective-permute-start.4
  162.4 4.5 collective-permute-done.5
  167.3 47.4 %all-gather.3 = f32[64,1,256]{2,1,0:T(1,128)S(1)} all-gather(f32[1,1,256]{2,1,0:T(1,128)S(1)} %bitcast.253), channel_id=1, replica_groups=mesh['roll'=64,'side'=8] {'roll'}, dimensions={0}, use_global_device_ids=true | all-gather | bytes 66560 | tf_op jit(solution)/shard_map/all_gather | solution.py:35
  215.0 4.9 %collective-permute-start.6 = (f32[128,1]{0,1:T(1,128)S(1)}, f32[128,1]{0,1:T(1,128)S(1)}, u32[]{:S(2)}, u32[]{:S(2)}) collective-permute-start(f32[128,1]{0,1:T(1,128)S(1)} %get-tuple-element.238), channel_id=1, source_target_pairs={{0,1},{1,2},{2,3},{3,4},{4,5},{5,6},{6,7},{8,9},{9,10},{10,11},{11... | collective-permute-start | bytes 1544 | tf_op jit(solution)/shard_map/ppermute | solution.py:24
  221.2 3.3 collective-permute-done.7
  224.9 45.1 %all-gather.4 = f32[64,1,256]{2,1,0:T(1,128)S(1)} all-gather(f32[1,1,256]{2,1,0:T(1,128)S(1)} %bitcast.254), channel_id=1, replica_groups=mesh['roll'=64,'side'=8] {'roll'}, dimensions={0}, use_global_device_ids=true | all-gather | bytes 66560 | tf_op jit(solution)/shard_map/all_gather | solution.py:35
  271.0 9.5 %all-to-all-start = ((f32[1,128,256]{2,0,1:T(1,128)}), f32[1,128,256]{2,0,1:T(1,128)S(1)}, u32[]{:S(2)}, u32[]{:S(2)}) async-start(f32[1,128,256]{2,0,1:T(1,128)} %copy.59), calls=%async_computation | async-start | bytes 262144 | tf_op jit(solution)/shard_map/all_to_all | solution.py:127
  280.5 10.4 %all-to-all-done = f32[1,128,256]{2,0,1:T(1,128)S(1)} async-done(((f32[1,128,256]{2,0,1:T(1,128)}), f32[1,128,256]{2,0,1:T(1,128)S(1)}, u32[]{:S(2)}, u32[]{:S(2)}) %all-to-all-start) | async-done | bytes 131104 | tf_op jit(solution)/shard_map/all_to_all | solution.py:127
  292.7 4.9 %all-to-all-start.1 = ((f32[128,2,256]{2,1,0:T(2,128)}), f32[128,2,256]{2,1,0:T(2,128)S(1)}, u32[]{:S(2)}, u32[]{:S(2)}) async-start(f32[128,2,256]{2,1,0:T(2,128)} %copy.61), calls=%async_computation.1 | async-start | bytes 524288 | tf_op jit(solution)/shard_map/all_to_all | solution.py:136
  299.7 9.8 %all-to-all-done.1 = f32[128,2,256]{2,1,0:T(2,128)S(1)} async-done(((f32[128,2,256]{2,1,0:T(2,128)}), f32[128,2,256]{2,1,0:T(2,128)S(1)}, u32[]{:S(2)}, u32[]{:S(2)}) %all-to-all-start.1) | async-done | bytes 262176 | tf_op jit(solution)/shard_map/all_to_all | solution.py:136
  309.6 16.8 %all-to-all-start.2 = ((f32[128,2,256]{2,1,0:T(2,128)}), f32[128,2,256]{2,1,0:T(2,128)S(1)}, u32[]{:S(2)}, u32[]{:S(2)}) async-start(f32[128,2,256]{2,1,0:T(2,128)} %copy.64), calls=%async_computation.2 | async-start | bytes 524288 | tf_op jit(solution)/shard_map/all_to_all | solution.py:137
  328.2 10.0 %all-to-all-done.2 = f32[128,2,256]{2,1,0:T(2,128)S(1)} async-done(((f32[128,2,256]{2,1,0:T(2,128)}), f32[128,2,256]{2,1,0:T(2,128)S(1)}, u32[]{:S(2)}, u32[]{:S(2)}) %all-to-all-start.2) | async-done | bytes 262176 | tf_op jit(solution)/shard_map/all_to_all | solution.py:137
  340.6 4.3 all-to-all-start.3
  347.1 8.6 %all-to-all-done.3 = f32[8,32,1,256]{3,1,2,0:T(8,128)S(1)} async-done(((f32[8,32,1,256]{3,1,2,0:T(8,128)}), f32[8,32,1,256]{3,1,2,0:T(8,128)S(1)}, u32[]{:S(2)}, u32[]{:S(2)}) %all-to-all-start.3) | async-done | bytes 262176 | tf_op jit(solution)/shard_map/all_to_all | solution.py:151
  355.7 3.4 all-to-all-start.4
  359.8 8.4 %all-to-all-done.4 = f32[8,32,1,256]{3,1,2,0:T(8,128)S(1)} async-done(((f32[8,32,1,256]{3,1,2,0:T(8,128)}), f32[8,32,1,256]{3,1,2,0:T(8,128)S(1)}, u32[]{:S(2)}, u32[]{:S(2)}) %all-to-all-start.4) | async-done | bytes 262176 | tf_op jit(solution)/shard_map/all_to_all | solution.py:154
  385.2 3.4 all-to-all-start.6
  390.4 7.6 %all-to-all-done.6 = f32[1,32,8,256]{3,1,0,2:T(8,128)S(1)} async-done(((f32[1,32,8,256]{3,1,0,2:T(8,128)}), f32[1,32,8,256]{3,1,0,2:T(8,128)S(1)}, u32[]{:S(2)}, u32[]{:S(2)}) %all-to-all-start.6) | async-done | bytes 262176 | tf_op jit(solution)/shard_map/all_to_all | solution.py:188
  398.1 3.4 all-to-all-start.5
  402.2 8.6 %all-to-all-done.5 = f32[1,32,8,256]{3,1,0,2:T(8,128)S(1)} async-done(((f32[1,32,8,256]{3,1,0,2:T(8,128)}), f32[1,32,8,256]{3,1,0,2:T(8,128)S(1)}, u32[]{:S(2)}, u32[]{:S(2)}) %all-to-all-start.5) | async-done | bytes 262176 | tf_op jit(solution)/shard_map/all_to_all | solution.py:187
  413.9 11.6 %all-to-all-start.7 = ((f32[2,128,256]{2,0,1:T(2,128)}), f32[2,128,256]{2,0,1:T(2,128)S(1)}, u32[]{:S(2)}, u32[]{:S(2)}) async-start(f32[2,128,256]{2,0,1:T(2,128)} %copy.76), calls=%async_computation.7 | async-start | bytes 524288 | tf_op jit(solution)/shard_map/all_to_all | solution.py:198
  426.4 11.1 %all-to-all-done.7 = f32[2,128,256]{2,0,1:T(2,128)S(1)} async-done(((f32[2,128,256]{2,0,1:T(2,128)}), f32[2,128,256]{2,0,1:T(2,128)S(1)}, u32[]{:S(2)}, u32[]{:S(2)}) %all-to-all-start.7) | async-done | bytes 262176 | tf_op jit(solution)/shard_map/all_to_all | solution.py:198
  437.5 6.4 %all-to-all-start.8 = ((f32[2,128,256]{2,0,1:T(2,128)}), f32[2,128,256]{2,0,1:T(2,128)S(1)}, u32[]{:S(2)}, u32[]{:S(2)}) async-start(f32[2,128,256]{2,0,1:T(2,128)} %copy.78), calls=%async_computation.8 | async-start | bytes 524288 | tf_op jit(solution)/shard_map/all_to_all | solution.py:199
  445.3 10.5 %all-to-all-done.8 = f32[2,128,256]{2,0,1:T(2,128)S(1)} async-done(((f32[2,128,256]{2,0,1:T(2,128)}), f32[2,128,256]{2,0,1:T(2,128)S(1)}, u32[]{:S(2)}, u32[]{:S(2)}) %all-to-all-start.8) | async-done | bytes 262176 | tf_op jit(solution)/shard_map/all_to_all | solution.py:199
  457.2 6.0 %all-to-all-start.9 = ((f32[64,2,256]{2,1,0:T(2,128)}), f32[64,2,256]{2,1,0:T(2,128)S(1)}, u32[]{:S(2)}, u32[]{:S(2)}) async-start(f32[64,2,256]{2,1,0:T(2,128)} %copy.80), calls=%async_computation.9 | async-start | bytes 262144 | tf_op jit(solution)/shard_map/all_to_all | solution.py:206
  464.2 9.4 %all-to-all-done.9 = f32[64,2,256]{2,1,0:T(2,128)S(1)} async-done(((f32[64,2,256]{2,1,0:T(2,128)}), f32[64,2,256]{2,1,0:T(2,128)S(1)}, u32[]{:S(2)}, u32[]{:S(2)}) %all-to-all-start.9) | async-done | bytes 131104 | tf_op jit(solution)/shard_map/all_to_all | solution.py:206
  (130 shorter events, 49.6 us)
Async XLA Ops:
  0.6 6.4 %copy-start = (f32[128,128]{1,0:T(8,128)S(1)}, f32[128,128]{1,0:T(8,128)}, u32[]{:S(2)}) copy-start(f32[128,128]{1,0:T(8,128)} %param.19) | copy-start | bytes 196612
  0.6 58.4 %copy-start.3 = (f32[128,256]{1,0:T(8,128)S(1)}, f32[128,256]{1,0:T(8,128)}, u32[]{:S(2)}) copy-start(f32[128,256]{1,0:T(8,128)} %param.17) | copy-start | bytes 393220
  1.6 57.3 %collective-permute-start = (f32[128,1]{1,0:T(8,128)S(1)}, f32[128,1]{1,0:T(8,128)S(1)}, u32[]{:S(2)}, u32[]{:S(2)}) collective-permute-start(f32[128,1]{1,0:T(8,128)S(1)} %get-tuple-element.244), channel_id=1, source_target_pairs={{0,1},{1,2},{2,3},{3,4},{4,5},{5,6},{6,7},{8,9},{9,10},{10,11},{11... | collective-permute-start | bytes 1544 | tf_op jit(solution)/shard_map/ppermute | solution.py:24
  5.7 2.0 copy-start.6
  5.7 2.0 copy-start.5
  5.7 53.3 %collective-permute-start.1 = (f32[128,1]{1,0:T(8,128)S(1)}, f32[128,1]{1,0:T(8,128)S(1)}, u32[]{:S(2)}, u32[]{:S(2)}) collective-permute-start(f32[128,1]{1,0:T(8,128)S(1)} %get-tuple-element.245), channel_id=1, source_target_pairs={{1,0},{2,1},{3,2},{4,3},{5,4},{6,5},{7,6},{9,8},{10,9},{11,10},{12... | collective-permute-start | bytes 1544 | tf_op jit(solution)/shard_map/ppermute | solution.py:26
  7.5 51.5 %copy-start.1 = (f32[128,256]{1,0:T(8,128)S(1)}, f32[128,256]{1,0:T(8,128)}, u32[]{:S(2)}) copy-start(f32[128,256]{1,0:T(8,128)} %param.16) | copy-start | bytes 393220
  7.5 51.5 %copy-start.2 = (f32[128,256]{1,0:T(8,128)S(1)}, f32[128,256]{1,0:T(8,128)}, u32[]{:S(2)}) copy-start(f32[128,256]{1,0:T(8,128)} %param.18) | copy-start | bytes 393220
  102.8 5.8 %collective-permute-start.2 = (f32[128,1]{0,1:T(1,128)S(1)}, f32[128,1]{0,1:T(1,128)S(1)}, u32[]{:S(2)}, u32[]{:S(2)}) collective-permute-start(f32[128,1]{0,1:T(1,128)S(1)} %get-tuple-element.242), channel_id=1, source_target_pairs={{0,1},{1,2},{2,3},{3,4},{4,5},{5,6},{6,7},{8,9},{9,10},{10,11},{11... | collective-permute-start | bytes 1544 | tf_op jit(solution)/shard_map/ppermute | solution.py:24
  107.1 4.3 collective-permute-start.3
  157.5 4.9 %collective-permute-start.4 = (f32[128,1]{0,1:T(1,128)S(1)}, f32[128,1]{0,1:T(1,128)S(1)}, u32[]{:S(2)}, u32[]{:S(2)}) collective-permute-start(f32[128,1]{0,1:T(1,128)S(1)} %get-tuple-element.240), channel_id=1, source_target_pairs={{0,1},{1,2},{2,3},{3,4},{4,5},{5,6},{6,7},{8,9},{9,10},{10,11},{11... | collective-permute-start | bytes 1544 | tf_op jit(solution)/shard_map/ppermute | solution.py:24
  161.1 5.8 %collective-permute-start.5 = (f32[128,1]{0,1:T(1,128)S(1)}, f32[128,1]{0,1:T(1,128)S(1)}, u32[]{:S(2)}, u32[]{:S(2)}) collective-permute-start(f32[128,1]{0,1:T(1,128)S(1)} %get-tuple-element.241), channel_id=1, source_target_pairs={{1,0},{2,1},{3,2},{4,3},{5,4},{6,5},{7,6},{9,8},{10,9},{11,10},{12... | collective-permute-start | bytes 1544 | tf_op jit(solution)/shard_map/ppermute | solution.py:26
  215.0 6.2 %collective-permute-start.6 = (f32[128,1]{0,1:T(1,128)S(1)}, f32[128,1]{0,1:T(1,128)S(1)}, u32[]{:S(2)}, u32[]{:S(2)}) collective-permute-start(f32[128,1]{0,1:T(1,128)S(1)} %get-tuple-element.238), channel_id=1, source_target_pairs={{0,1},{1,2},{2,3},{3,4},{4,5},{5,6},{6,7},{8,9},{9,10},{10,11},{11... | collective-permute-start | bytes 1544 | tf_op jit(solution)/shard_map/ppermute | solution.py:24
  219.9 4.6 collective-permute-start.7
  271.0 19.8 %all-to-all-start = ((f32[1,128,256]{2,0,1:T(1,128)}), f32[1,128,256]{2,0,1:T(1,128)S(1)}, u32[]{:S(2)}, u32[]{:S(2)}) async-start(f32[1,128,256]{2,0,1:T(1,128)} %copy.59), calls=%async_computation | async-start | bytes 262144 | tf_op jit(solution)/shard_map/all_to_all | solution.py:127
  292.7 16.9 %all-to-all-start.1 = ((f32[128,2,256]{2,1,0:T(2,128)}), f32[128,2,256]{2,1,0:T(2,128)S(1)}, u32[]{:S(2)}, u32[]{:S(2)}) async-start(f32[128,2,256]{2,1,0:T(2,128)} %copy.61), calls=%async_computation.1 | async-start | bytes 524288 | tf_op jit(solution)/shard_map/all_to_all | solution.py:136
  309.6 28.6 %all-to-all-start.2 = ((f32[128,2,256]{2,1,0:T(2,128)}), f32[128,2,256]{2,1,0:T(2,128)S(1)}, u32[]{:S(2)}, u32[]{:S(2)}) async-start(f32[128,2,256]{2,1,0:T(2,128)} %copy.64), calls=%async_computation.2 | async-start | bytes 524288 | tf_op jit(solution)/shard_map/all_to_all | solution.py:137
  340.6 15.1 %all-to-all-start.3 = ((f32[8,32,1,256]{3,1,2,0:T(8,128)}), f32[8,32,1,256]{3,1,2,0:T(8,128)S(1)}, u32[]{:S(2)}, u32[]{:S(2)}) async-start(f32[8,32,1,256]{3,1,2,0:T(8,128)} %bitcast.35), calls=%async_computation.3 | async-start | bytes 524288 | tf_op jit(solution)/shard_map/all_to_all | solution.py:151
  355.7 12.6 %all-to-all-start.4 = ((f32[8,32,1,256]{3,1,2,0:T(8,128)}), f32[8,32,1,256]{3,1,2,0:T(8,128)S(1)}, u32[]{:S(2)}, u32[]{:S(2)}) async-start(f32[8,32,1,256]{3,1,2,0:T(8,128)} %bitcast.42), calls=%async_computation.4 | async-start | bytes 524288 | tf_op jit(solution)/shard_map/all_to_all | solution.py:154
  385.2 12.8 %all-to-all-start.6 = ((f32[1,32,8,256]{3,1,0,2:T(8,128)}), f32[1,32,8,256]{3,1,0,2:T(8,128)S(1)}, u32[]{:S(2)}, u32[]{:S(2)}) async-start(f32[1,32,8,256]{3,1,0,2:T(8,128)} %copy.72), calls=%async_computation.6 | async-start | bytes 524288 | tf_op jit(solution)/shard_map/all_to_all | solution.py:188
  398.1 12.8 %all-to-all-start.5 = ((f32[1,32,8,256]{3,1,0,2:T(8,128)}), f32[1,32,8,256]{3,1,0,2:T(8,128)S(1)}, u32[]{:S(2)}, u32[]{:S(2)}) async-start(f32[1,32,8,256]{3,1,0,2:T(8,128)} %copy.70), calls=%async_computation.5 | async-start | bytes 524288 | tf_op jit(solution)/shard_map/all_to_all | solution.py:187
  413.9 23.6 %all-to-all-start.7 = ((f32[2,128,256]{2,0,1:T(2,128)}), f32[2,128,256]{2,0,1:T(2,128)S(1)}, u32[]{:S(2)}, u32[]{:S(2)}) async-start(f32[2,128,256]{2,0,1:T(2,128)} %copy.76), calls=%async_computation.7 | async-start | bytes 524288 | tf_op jit(solution)/shard_map/all_to_all | solution.py:198
  437.5 18.3 %all-to-all-start.8 = ((f32[2,128,256]{2,0,1:T(2,128)}), f32[2,128,256]{2,0,1:T(2,128)S(1)}, u32[]{:S(2)}, u32[]{:S(2)}) async-start(f32[2,128,256]{2,0,1:T(2,128)} %copy.78), calls=%async_computation.8 | async-start | bytes 524288 | tf_op jit(solution)/shard_map/all_to_all | solution.py:199
  457.2 16.4 %all-to-all-start.9 = ((f32[64,2,256]{2,1,0:T(2,128)}), f32[64,2,256]{2,1,0:T(2,128)S(1)}, u32[]{:S(2)}, u32[]{:S(2)}) async-start(f32[64,2,256]{2,1,0:T(2,128)} %copy.80), calls=%async_computation.9 | async-start | bytes 262144 | tf_op jit(solution)/shard_map/all_to_all | solution.py:206
  464.2 9.5 %copy-start.4 = (s32[128,256]{1,0:T(8,128)S(1)}, s32[128,256]{1,0:T(8,128)}, u32[]{:S(2)}) copy-start(s32[128,256]{1,0:T(8,128)} %param.22) | copy-start | bytes 393220
where the time goes:
time: 483 us; the launch traced here: 475 us
  blocking collectives  231 us (48%)
  waiting for transfers between devices  105 us (22%)
  starting transfers between devices  91.6 us (19%)
  matrix products  28.2 us (6%)
  local copies, waits for them, and re-layouts  11.7 us (2%)
    all_gather x5, blocking collectives, entering(): gathered = jax.tree.map(lambda a: lax.all_gather(a, axis), part)  231 us
    all_to_all x1, starting transfers between devices, per_device(): lax.all_to_all(out_im, 'roll', split_axis=0, concat_axis=1, tiled=True)  16.8 us
    ppermute x4, starting transfers between devices, padded_2(): lax.ppermute(tail, axis, [(i, (i + 1) % count) for i in range(ends)])  16.7 us
    all_to_all x1, starting transfers between devices, per_device(): lax.all_to_all(line_re, 'roll', split_axis=1, concat_axis=0, tiled=True)  11.6 us
    all_to_all x1, waiting for transfers between devices, per_device(): lax.all_to_all(line_re, 'roll', split_axis=1, concat_axis=0, tiled=True)  11.1 us
    all_to_all x1, waiting for transfers between devices, per_device(): lax.all_to_all(line_im, 'roll', split_axis=1, concat_axis=0, tiled=True)  10.5 us
    ppermute x4, waiting for transfers between devices, padded_2(): lax.ppermute(head, axis, [((i + 1) % count, i) for i in range(ends)])  10.5 us
    all_to_all x1, waiting for transfers between devices, per_device(): lax.all_to_all(pressure_now[None], 'roll', split_axis=1, concat_axis=0, t...  10.4 us
  transfers between devices with their start and end apart: 18, of which 13 were waited for; matrix products, arithmetic and copies ran while one was open for 3% of the time, Pallas kernels for 0%

commit v1 on v0

v1 whole, which is shorter than its diff:
```python
import functools
import math

import jax
import jax.numpy as jnp
import ml_dtypes
import numpy as np
from jax import lax
from jax.experimental import pallas as pl
from jax.experimental.pallas import tpu as pltpu
from jax.sharding import PartitionSpec as P

SWEEPS = 4
ROUGH_STEP = 0.05
MESH = pl.DeviceIdType.MESH
F32 = jnp.float32
BF16 = jnp.bfloat16

N_ROLL, N_SIDE = 64, 8
ROWS, COLS = 128, 256
FFT_X, FFT_Y = 2 * N_ROLL * ROWS, 2 * N_SIDE * COLS
CLASSES = N_SIDE + 1


def split_np(x):
    x = x.astype(np.float32)
    hi = x.astype(ml_dtypes.bfloat16)
    lo = (x - hi.astype(np.float32)).astype(ml_dtypes.bfloat16)
    return hi, lo


def wide_np(x, axis):
    hi, lo = split_np(x)
    return np.concatenate([hi, hi, lo], axis=axis)


def turns(ints, length):
    return 2.0 * np.pi * (ints % length).astype(np.float64) / length


@functools.lru_cache(None)
def tables():
    a = np.arange(N_ROLL)
    ang = turns(a[:, None] * a[None, :], 2 * N_ROLL)
    sect = np.stack([np.cos(ang), -np.sin(ang)], axis=1)
    sect[0, 1] = np.where(a % 2 == 0, 1.0, -1.0)
    sect = np.einsum("uca,ij->uciaj", sect, np.eye(4)).reshape(8 * N_ROLL, 4 * N_ROLL)
    c = np.arange(COLS)
    ang = turns(c[:, None] * c[None, :], COLS)
    dcos, dsin = np.cos(ang), np.sin(ang)
    dft = np.block([[dcos, -dsin], [dsin, dcos]])
    v1 = np.arange(16)
    ang = turns(v1[:, None] * c[None, :], FFT_Y)
    twiddle = np.stack([np.cos(ang), np.sin(ang)]).astype(np.float32)
    q = np.arange(ROWS).reshape(N_SIDE, 16)
    t = np.arange(ROWS).reshape(32, 4)
    ang = turns(q[:, :, None, None] * t[None, None], ROWS)
    cb, sb = np.cos(ang), np.sin(ang)
    main = np.zeros((2, 2, N_SIDE, 2, 16, 32, 2, 4))
    main[1, 0, :, 0, :, :, 0], main[1, 0, :, 0, :, :, 1] = cb, sb
    main[1, 0, :, 1, :, :, 0], main[1, 0, :, 1, :, :, 1] = -sb, cb
    main[1, 1, :, 0, :, :, 0], main[1, 1, :, 0, :, :, 1] = -sb, cb
    main[1, 1, :, 1, :, :, 0], main[1, 1, :, 1, :, :, 1] = -cb, -sb
    even = np.where(q <= 64, q, q - 64)
    ang = turns(even[:, :, None, None] * t[None, None], ROWS)
    main[0, 0, :, 0, :, :, 0] = np.where((q <= 64)[:, :, None, None], np.cos(ang), np.sin(ang))
    odd = 64 + 128 * np.where(q < 64, q, q - 64)
    ang = turns(odd[:, :, None, None] * t[None, None], FFT_X)
    main[0, 0, :, 1, :, :, 1] = np.where((q < 64)[:, :, None, None], np.cos(ang), np.sin(ang))
    main = main.reshape(2, 2, 256, 256).astype(np.float32)
    cols_t = np.broadcast_to(t[:, None, :], (32, 2, 4)).reshape(256)
    ang = turns(a[:, None] * cols_t[None, :], FFT_X)
    slant = np.stack([np.cos(ang), np.sin(ang)], axis=1).astype(np.float32)
    return (
        wide_np(sect, 1),
        wide_np(sect.T, 1),
        wide_np(dft, 0),
        wide_np(dft.T, 0),
        main,
        slant,
        twiddle,
    )


def split(x):
    hi = x.astype(BF16)
    return hi, (x - hi.astype(F32)).astype(BF16)


def mm(a, b):
    return jnp.dot(a, b, preferred_element_type=F32)


def place(device):
    return lax.rem(device, 2) * 32 + lax.div(device, 2)


def combine(terms):
    total = None
    for coef, value in terms:
        if abs(coef) < 1e-12:
            continue
        if abs(coef - 1.0) < 1e-12:
            total = value if total is None else total + value
        elif abs(coef + 1.0) < 1e-12:
            total = -value if total is None else total - value
        else:
            total = coef * value if total is None else total + coef * value
    return total


def main_kernel(
    press, source, coupling, binv, lower, mask, rough, offset,
    w3_h, wt3_h, d3_h, dt3_h, main_h, slant_h, twid_h,
    newp, film,
    w3, wt3, d3, dt3, maint, slant, twid,
    pack, halo, bhalo,
    outs0, outs, recv0, recv, carry_buf,
    b3, be3,
    kern, m3, mt3,
    p1s, p1r, q3, p2s, p2r, x3, us, yb, zs, ob, ub, p5s, p5r, v3, p6s, p6r,
    const_sem, halo_ss, halo_rs, ss, rs,
):
    me = lax.axis_index("roll")
    side = lax.axis_index("side")
    barrier = pltpu.get_barrier_semaphore()

    def sig_roll(d, _):
        pl.semaphore_signal(
            barrier, inc=1, device_id={"roll": lax.rem(me + d, N_ROLL)}, device_id_type=MESH
        )
        return 0

    def sig_side(d, _):
        pl.semaphore_signal(
            barrier, inc=1, device_id={"side": lax.rem(side + d, N_SIDE)}, device_id_type=MESH
        )
        return 0

    lax.fori_loop(1, N_SIDE, sig_side, 0)
    lax.fori_loop(1, N_ROLL, sig_roll, 0)

    variant = jnp.minimum(me, 1)
    loads = [
        pltpu.make_async_copy(s, d, const_sem.at[i])
        for i, (s, d) in enumerate(
            [
                (w3_h, w3), (wt3_h, wt3), (d3_h, d3), (dt3_h, dt3),
                (main_h.at[variant], maint), (slant_h.at[me], slant), (twid_h, twid),
            ]
        )
    ]
    for load in loads:
        load.start()

    def send_all(axis, n, mine, src_at, dst_at, phase):
        def body(d, _):
            to = lax.rem(mine + d, n)
            pltpu.make_async_remote_copy(
                src_ref=src_at(to), dst_ref=dst_at(mine), send_sem=ss.at[phase],
                recv_sem=rs.at[phase], device_id={axis: to}, device_id_type=MESH,
            ).start()
            return 0

        lax.fori_loop(1, n, body, 0)

    def wait_all(axis, n, mine, src, dst, phase):
        c = pltpu.make_async_remote_copy(
            src_ref=src, dst_ref=dst, send_sem=ss.at[phase], recv_sem=rs.at[phase],
            device_id={axis: lax.rem(mine + 1, n)}, device_id_type=MESH,
        )
        c.wait()

    lane_b = lax.broadcasted_iota(jnp.int32, (ROWS, 128), 1)
    for i, ref in enumerate((press, source, coupling)):
        pack[0, pl.ds(8 * i, 8), :] = ref[:, 0:128].T[0:8]
        pack[1, pl.ds(8 * i, 8), :] = ref[:, 128:256].T[120:128]
    for j in range(2):
        lanes = slice(128 * j, 128 * j + 128)
        pack[j, pl.ds(24, 8), :] = jnp.concatenate(
            [lower[:, lanes], mask[:, lanes].astype(F32), jnp.zeros((6, 128), F32)], axis=0
        )
    pl.semaphore_wait(barrier, N_ROLL + N_SIDE - 2)
    halo_copies = []
    for j, d in ((0, N_SIDE - 1), (1, 1)):
        to = lax.rem(side + d, N_SIDE)
        for k, (s, dst) in enumerate(((pack.at[j], halo.at[j]), (binv, bhalo.at[j]))):
            c = pltpu.make_async_remote_copy(
                src_ref=s, dst_ref=dst, send_sem=halo_ss.at[j, k], recv_sem=halo_rs.at[j, k],
                device_id={"side": to}, device_id_type=MESH,
            )
            c.start()
            halo_copies.append(c)
    bhi, blo = split(binv[...])
    b3[:, 0:128] = bhi
    b3[:, 128:256] = bhi
    b3[:, 256:384] = blo
    for c in halo_copies:
        c.wait()
    has_right = side < N_SIDE - 1
    has_left = side > 0
    is_right = lane_b < 64
    valid = jnp.logical_or(
        jnp.logical_and(is_right, has_right), jnp.logical_and(jnp.logical_not(is_right), has_left)
    )
    ext = []
    for i in range(3):
        tall = jnp.concatenate(
            [halo[0, pl.ds(8 * i, 8), :], jnp.zeros((112, 128), F32), halo[1, pl.ds(8 * i, 8), :]],
            axis=0,
        )
        ext.append(jnp.where(valid, tall.T, 0.0))
    row_right = is_right[0:1]
    row_valid = valid[0:1]
    lower_e = jnp.where(row_valid, jnp.where(row_right, halo[0, 24:25, :], halo[1, 24:25, :]), 0.0)
    mask_e = jnp.where(row_right, halo[0, 25:26, :], halo[1, 25:26, :]) > 0.5
    rhi, rlo = split(bhalo[0])
    lhi, llo = split(bhalo[1])
    for i, part in enumerate((rhi, lhi, rhi, lhi, rlo, llo)):
        be3[:, pl.ds(128 * i, 128)] = part
    first_e = jnp.where(is_right, bhalo[0, :, 0:1], bhalo[1, :, 0:1])
    first = binv[:, 0:1]
    gain_e = first_e[127:128] * lower_e
    gain_m = binv[127:128, 0:1] * lower[...]
    lower_w = jnp.concatenate([lower[...], lower_e], axis=1)
    mask_w = jnp.concatenate([mask[...].astype(F32), mask_e.astype(F32)], axis=1) > 0.5
    first_w = jnp.concatenate([jnp.broadcast_to(first, (ROWS, COLS)), first_e], axis=1)
    source_w = jnp.concatenate([source[...], ext[1]], axis=1)
    coupling_w = jnp.concatenate([coupling[...], ext[2]], axis=1)
    field = jnp.concatenate([press[...], ext[0]], axis=1)
    for i in range(3):
        gi = gain_e if i == 2 else gain_m[:, 128 * i : 128 * i + 128]
        outs0[1, i : i + 1, :] = gi

    for sweep in range(SWEEPS):
        rhs = source_w + coupling_w * (pltpu.roll(field, 1, 1) + pltpu.roll(field, 383, 1))
        hi, lo = split(rhs)
        stack = jnp.concatenate([hi[:, :256], lo[:, :256], hi[:, :256]], axis=0)
        he, le = rhs[:, 256:], None
        hr, lr = split(jnp.where(is_right, he, 0.0))
        hl, ll = split(jnp.where(is_right, 0.0, he))
        stack_e = jnp.concatenate([hr, hl, lr, ll, hr, hl], axis=0)
        tail = mm(b3[112:128, :], stack)
        tail_e = mm(be3[112:128, :], stack_e)
        for i in range(3):
            row = tail_e[15:16] if i == 2 else tail[15:16, 128 * i : 128 * i + 128]
            if sweep == 0:
                outs0[0, i : i + 1, :] = row
            else:
                outs[sweep - 1, i : i + 1, :] = row
        if sweep == 0:
            send_all("roll", N_ROLL, me, lambda to: outs0, lambda m: recv0.at[m], 0)
        else:
            send_all(
                "roll", N_ROLL, me, lambda to: outs.at[sweep - 1],
                lambda m: recv.at[sweep - 1, m], sweep,
            )
        local = jnp.concatenate([mm(b3[...], stack), mm(be3[...], stack_e)], axis=1)
        if sweep == 0:
            i = lax.broadcasted_iota(jnp.int32, (32, COLS), 0)
            q = 16 * side + jnp.where(i < 16, i, i - 16)
            low_part = i < 16
            u_even = 128 * jnp.where(q <= 64, q, q - 64)
            u_odd = 64 + 128 * jnp.where(q < 64, q, q - 64)
            u = jnp.where(me == 0, jnp.where(low_part, u_even, u_odd), me + 128 * q)
            fu = jnp.minimum(u, FFT_X - u).astype(F32) / FFT_X
            single = jnp.logical_and(
                jnp.logical_and(me == 0, low_part), jnp.logical_or(q == 0, q == 64)
            )
            reach = min(FFT_X, FFT_Y) / 16.0
            scale = 0.4 * reach / (float(FFT_X) * float(FFT_Y))
            weight = jnp.where(single, scale, 2.0 * scale)
            fu2 = fu * fu
            lane = lax.broadcasted_iota(jnp.int32, (32, COLS), 1)
            for v1 in range(CLASSES):
                v = v1 + 16 * lane
                fv = jnp.minimum(v, FFT_Y - v).astype(F32) / FFT_Y
                w = weight if v1 in (0, 8) else 2.0 * weight
                kern[pl.ds(32 * v1, 32), :] = w / (1.0 + reach * jnp.sqrt(fu2 + fv * fv))
        if sweep == 1:
            loads[4].wait()
            loads[5].wait()
            mrow = maint[0] * slant[0:1, :] + maint[1] * slant[1:2, :]
            hi, lo = split(mrow)
            m3[:, 0:256] = hi
            m3[:, 256:512] = hi
            m3[:, 512:768] = lo
        if sweep == 2:
            mrow = maint[0] * slant[0:1, :] + maint[1] * slant[1:2, :]
            hi, lo = split(mrow.T)
            mt3[:, 0:256] = hi
            mt3[:, 256:512] = hi
            mt3[:, 512:768] = lo
        if sweep == 0:
            wait_all(
                "roll", N_ROLL, me, recv0.at[pl.ds(0, N_ROLL - 1)],
                recv0.at[pl.ds(0, N_ROLL - 1)], 0,
            )
        else:
            sl = recv.at[sweep - 1, pl.ds(0, N_ROLL - 1)]
            wait_all("roll", N_ROLL, me, sl, sl, sweep)

        def advance(k8, c):
            for j in range(8):
                k = 8 * k8 + j
                carry_buf[k] = c
                flow = recv0[k, 0] if sweep == 0 else recv[sweep - 1, k]
                c = flow + recv0[k, 1] * c
            return c

        lax.fori_loop(0, N_ROLL // 8, advance, jnp.zeros((3, 128), F32))
        mine = carry_buf[me]
        carry = jnp.concatenate([mine[0:1], mine[1:2], mine[2:3]], axis=1)
        solved = local + first_w * (lower_w * carry)
        field = jnp.where(mask_w, jnp.maximum(solved, 0.0), solved)

    result = field[:, :COLS]
    newp[...] = result

    for h in range(2):
        p1s[pl.ds(32 * h, 32)] = result[:, 128 * h : 128 * h + 128].reshape(32, 4, 128)
    send_all("roll", N_ROLL, me, lambda to: p1s.at[place(to)], lambda m: p1r.at[m], 4)
    p1r[me] = p1s[place(me)]
    loads[0].wait()
    wait_all("roll", N_ROLL, me, p1s.at[pl.ds(0, 63)], p1r.at[pl.ds(0, 63)], 4)
    hi, lo = split(p1r[...].reshape(256, 128))
    q3[0:256] = hi
    q3[256:512] = lo
    q3[512:768] = hi
    p2s[...] = mm(w3[...], q3[...]).reshape(64, 8, 128)

    send_all("roll", N_ROLL, me, lambda to: p2s.at[to], lambda m: p2r.at[place(m)], 5)
    p2r[place(me)] = p2s[me]
    wait_all("roll", N_ROLL, me, p2s.at[pl.ds(0, 63)], p2r.at[pl.ds(0, 63)], 5)
    for h in range(2):
        hi, lo = split(p2r[pl.ds(32 * h, 32)].reshape(256, 128))
        lanes = slice(128 * h, 128 * h + 128)
        x3[0:256, lanes] = hi
        x3[256:512, lanes] = lo
        x3[512:768, lanes] = hi
    us[...] = mm(m3[...], x3[...]).reshape(8, 32, 256)

    send_all("side", N_SIDE, side, lambda to: us.at[to], lambda m: yb.at[m], 6)
    yb[side] = us[side]
    loads[2].wait()
    loads[3].wait()
    loads[6].wait()
    wait_all("side", N_SIDE, side, us.at[pl.ds(0, 7)], yb.at[pl.ds(0, 7)], 6)

    cosines = [[math.cos(math.pi * s * v / 8.0) for v in range(9)] for s in range(8)]
    sines = [[math.sin(math.pi * s * v / 8.0) for v in range(9)] for s in range(8)]

    def put(v1, rows, lanes, re, im):
        at = 32 * v1 + rows
        for part, value in ((0, re), (256, im)):
            hi, lo = split(value)
            zs[pl.ds(at, 16), pl.ds(part + lanes, 128)] = hi
            zs[pl.ds(at, 16), pl.ds(512 + part + lanes, 128)] = lo
            zs[pl.ds(at, 16), pl.ds(1024 + part + lanes, 128)] = hi

    for rows in (0, 16):
        for lanes in (0, 128):
            x = [yb[s, pl.ds(rows, 16), pl.ds(lanes, 128)] for s in range(8)]
            for v in range(5):
                er = combine([(cosines[s][v], x[s]) for s in (0, 2, 4, 6)])
                orr = combine([(cosines[s][v], x[s]) for s in (1, 3, 5, 7)])
                ei = combine([(-sines[s][v], x[s]) for s in (0, 2, 4, 6)])
                oi = combine([(-sines[s][v], x[s]) for s in (1, 3, 5, 7)])
                zero = jnp.zeros((16, 128), F32)
                ei = zero if ei is None else ei
                oi = zero if oi is None else oi
                orr = zero if orr is None else orr
                todo = [(v, er + orr, ei + oi)]
                if v < 4:
                    todo.append((8 - v, er - orr, oi - ei))
                for v1, yr, yi in todo:
                    c = twid[0, v1 : v1 + 1, lanes : lanes + 128]
                    s = twid[1, v1 : v1 + 1, lanes : lanes + 128]
                    put(v1, rows, lanes, yr * c + yi * s, yi * c - yr * s)
    spec = mm(zs[...], d3[...])
    for v1 in range(CLASSES):
        for rows in (0, 16):
            at = 32 * v1 + rows
            for lanes in (0, 128):
                k = kern[pl.ds(at, 16), pl.ds(lanes, 128)]
                put(
                    v1, rows, lanes,
                    spec[at : at + 16, lanes : lanes + 128] * k,
                    spec[at : at + 16, 256 + lanes : 384 + lanes] * k,
                )
    back = mm(zs[...], dt3[...])
    for rows in (0, 16):
        for lanes in (0, 128):
            yr, yi = [], []
            for v1 in range(CLASSES):
                at = 32 * v1 + rows
                zr = back[at : at + 16, lanes : lanes + 128]
                zi = back[at : at + 16, 256 + lanes : 384 + lanes]
                c = twid[0, v1 : v1 + 1, lanes : lanes + 128]
                s = twid[1, v1 : v1 + 1, lanes : lanes + 128]
                yr.append(zr * c - zi * s)
                yi.append(zr * s + zi * c)
            plus_r = [yr[v] + yr[8 - v] for v in range(4)] + [yr[4]]
            plus_i = [yi[v] + yi[8 - v] for v in range(4)] + [yi[4]]
            less_r = [yr[v] - yr[8 - v] for v in range(4)] + [yr[4]]
            less_i = [yi[v] - yi[8 - v] for v in range(4)] + [yi[4]]
            for s in range(8):
                re, im = (plus_r, less_i) if s % 2 == 0 else (less_r, plus_i)
                ob[s, pl.ds(rows, 16), pl.ds(lanes, 128)] = combine(
                    [(cosines[s][v], re[v]) for v in range(5)]
                    + [(-sines[s][v], im[v]) for v in range(5)]
                )

    send_all("side", N_SIDE, side, lambda to: ob.at[to], lambda m: ub.at[m], 7)
    ub[side] = ob[side]
    wait_all("side", N_SIDE, side, ob.at[pl.ds(0, 7)], ub.at[pl.ds(0, 7)], 7)
    hi, lo = split(ub[...].reshape(256, 256))
    x3[0:256] = hi
    x3[256:512] = lo
    x3[512:768] = hi
    rows_back = mm(mt3[...], x3[...])
    for h in range(2):
        p5s[pl.ds(32 * h, 32)] = rows_back[:, 128 * h : 128 * h + 128].reshape(32, 8, 128)

    send_all("roll", N_ROLL, me, lambda to: p5s.at[place(to)], lambda m: p5r.at[m], 8)
    p5r[me] = p5s[place(me)]
    loads[1].wait()
    wait_all("roll", N_ROLL, me, p5s.at[pl.ds(0, 63)], p5r.at[pl.ds(0, 63)], 8)
    hi, lo = split(p5r[...].reshape(512, 128))
    v3[0:512] = hi
    v3[512:1024] = lo
    v3[1024:1536] = hi
    p6s[...] = mm(wt3[...], v3[...]).reshape(64, 4, 128)

    send_all("roll", N_ROLL, me, lambda to: p6s.at[to], lambda m: p6r.at[place(m)], 9)
    p6r[place(me)] = p6s[me]
    row_pos = (me * ROWS + lax.broadcasted_iota(jnp.int32, (ROWS, COLS), 0)).astype(F32)
    col_pos = (side * COLS + lax.broadcasted_iota(jnp.int32, (ROWS, COLS), 1)).astype(F32)
    across = 4.0 * (row_pos + 0.5) / (ROWS * N_ROLL) - 2.5
    transverse = 4.0 * (col_pos + 0.5) / (COLS * N_SIDE) - 2.0
    ground = offset[0] + 0.5 * across * across + 0.5 * transverse * transverse
    ripple = ROUGH_STEP * rough[...].astype(F32)
    wait_all("roll", N_ROLL, me, p6s.at[pl.ds(0, 63)], p6r.at[pl.ds(0, 63)], 9)
    for h in range(2):
        lanes = slice(128 * h, 128 * h + 128)
        bend = p6r[pl.ds(32 * h, 32)].reshape(128, 128)
        film[:, lanes] = ground[:, lanes] + bend - ripple[:, lanes]


def per_device(pressure, source, coupling, binv, lower, mask, rough, offset):
    consts = [jnp.asarray(t) for t in tables()]
    vm = pl.BlockSpec(memory_space=pltpu.VMEM)
    hbm = pl.BlockSpec(memory_space=pl.ANY)
    f = lambda *shape: pltpu.VMEM(shape, F32)
    b = lambda *shape: pltpu.VMEM(shape, BF16)
    scratch = [
        b(512, 768), b(256, 1536), b(1536, 512), b(1536, 512),
        f(2, 256, 256), f(2, 256), f(2, 16, 256),
        f(2, 32, 128), f(2, 32, 128), f(2, 128, 128),
        f(2, 3, 128), f(3, 3, 128), f(64, 2, 3, 128), f(3, 64, 3, 128), f(64, 3, 128),
        b(128, 384), b(128, 768),
        f(288, 256), b(256, 768), b(256, 768),
        f(64, 4, 128), f(64, 4, 128), b(768, 128), f(64, 8, 128), f(64, 8, 128), b(768, 256),
        f(8, 32, 256), f(8, 32, 256), b(288, 1536), f(8, 32, 256), f(8, 32, 256),
        f(64, 8, 128), f(64, 8, 128), b(1536, 128), f(64, 4, 128), f(64, 4, 128),
        pltpu.SemaphoreType.DMA((7,)),
        pltpu.SemaphoreType.DMA((2, 2)), pltpu.SemaphoreType.DMA((2, 2)),
        pltpu.SemaphoreType.DMA((10,)), pltpu.SemaphoreType.DMA((10,)),
    ]
    out = jax.ShapeDtypeStruct((ROWS, COLS), F32)
    return pl.pallas_call(
        main_kernel,
        out_shape=(out, out),
        in_specs=[vm] * 7 + [pl.BlockSpec(memory_space=pltpu.SMEM)] + [hbm] * 7,
        out_specs=(vm, vm),
        scratch_shapes=scratch,
        compiler_params=pltpu.CompilerParams(
            collective_id=0, has_side_effects=True, vmem_limit_bytes=40 * 1024 * 1024
        ),
    )(pressure, source, coupling, binv, lower, mask, rough, offset, *consts)


def solution(mesh):
    spec = P("roll", "side")
    return jax.shard_map(
        per_device,
        mesh=mesh,
        in_specs=(spec,) * 7 + (P(),),
        out_specs=(spec, spec),
        check_vma=False,
    )
```

time: 483 us -> 121 us (0.25); the launches traced: 475 us -> 119 us
  blocking collectives: 231 us -> 0 us
  waiting for transfers between devices: 105 us -> 0 us
  Pallas kernels: 0 us -> 103 us
  starting transfers between devices: 91.6 us -> 0 us
  matrix products: 28.2 us -> 0 us
    all_gather x5 -> x0, blocking collectives: 231 us -> none  [entering(): gathered = jax.tree.map(lambda a: lax.all_gather(a, axis), part)]
    pallas_call x0 -> x1, Pallas kernels: none -> 103 us  [per_device(): pl.pallas_call(main_kernel, out_shape=(out, out), in_specs=[vm] * 7 + [pl...]
    all_to_all x10 -> x0, waiting for transfers between devices: 94.6 us -> none  [the longest x1 11.1 us: per_device(): lax.all_to_all(line_re, 'roll', split_axis=1, concat_axis=0, tiled=True)]
    all_to_all x10 -> x0, starting transfers between devices: 69.7 us -> none  [the longest x1 16.8 us: per_device(): lax.all_to_all(out_im, 'roll', split_axis=0, concat_axis=1, tiled=True)]
    dot_general x32 -> x0, matrix products: 28.2 us -> none  [the longest x6 6.78 us: complex_product(): jnp.einsum(formula, left_im, right_re, precision=HIGHEST)]
    ppermute x8 -> x0, starting transfers between devices: 21.9 us -> none  [the longest x4 16.7 us: padded_2(): lax.ppermute(tail, axis, [(i, (i + 1) % count) for i in range(ends)])]
    unnamed x22 -> x30, local copies, waits for them, and re-layouts: 1 us -> 15.1 us
    ppermute x8 -> x0, waiting for transfers between devices: 10.5 us -> none  [the longest x4 10.5 us: padded_2(): lax.ppermute(head, axis, [((i + 1) % count, i) for i in range(ends)])]
  transfers between devices with their start and end apart: 18 -> 0, of which waited for: 13 -> 0; matrix products, arithmetic and copies ran while one was open for 3% -> 0% of each run, Pallas kernels for 0% -> 0%
where the time goes in v1:
time: 121 us; the launch traced here: 119 us
  Pallas kernels  103 us (85%)
  local copies, waits for them, and re-layouts  15.1 us (12%)
  between operations  1.31 us (1%)
    pallas_call x1, Pallas kernels, per_device(): pl.pallas_call(main_kernel, out_shape=(out, out), in_specs=[vm] * 7 + [pl...  103 us
    unnamed x30, local copies, waits for them, and re-layouts  15.1 us

profile of v1, /device:TPU:1, one launch (start us, length us, event | category | flops | bytes accessed | tf_op | source)
XLA Modules:
  0.0 119.2 jit_solution(7120319790953156370)
XLA Ops:
  1.3 0.0 copy-start
  1.3 1.4 %copy-done = bf16[1536,512]{1,0:T(8,128)(2,1)S(1)} copy-done((bf16[1536,512]{1,0:T(8,128)(2,1)S(1)}, bf16[1536,512]{1,0:T(8,128)(2,1)}, u32[]{:S(2)}) %copy-start) | copy-done | bytes 1572888
  2.7 0.0 copy-start.1
  2.7 1.4 %copy-done.1 = bf16[1536,512]{1,0:T(8,128)(2,1)S(1)} copy-done((bf16[1536,512]{1,0:T(8,128)(2,1)S(1)}, bf16[1536,512]{1,0:T(8,128)(2,1)}, u32[]{:S(2)}) %copy-start.1) | copy-done | bytes 1572888
  4.1 0.0 copy-start.2
  4.1 1.2 %copy-done.2 = f32[2,2,256,256]{3,2,1,0:T(8,128)S(1)} copy-done((f32[2,2,256,256]{3,2,1,0:T(8,128)S(1)}, f32[2,2,256,256]{3,2,1,0:T(8,128)}, u32[]{:S(2)}) %copy-start.2) | copy-done | bytes 1048600
  5.3 0.0 copy-start.3
  5.3 1.1 copy-done.3
  6.5 0.0 copy-start.4
  6.5 1.1 copy-done.4
  7.6 0.0 copy-start.5
  7.6 0.9 copy-done.5
  8.5 0.0 copy-start.6
  8.5 0.9 copy-done.6
  9.4 0.0 copy-start.7
  9.4 0.9 copy-done.7
  10.3 0.0 copy-start.8
  10.3 0.9 copy-done.8
  11.2 0.0 copy-start.9
  11.2 0.9 copy-done.9
  12.1 0.0 copy-start.10
  12.1 0.8 copy-done.10
  13.0 0.0 copy-start.11
  13.0 0.8 copy-done.11
  13.7 0.0 copy-start.12
  13.7 0.7 copy-done.12
  14.4 0.0 copy-start.13
  14.4 0.7 copy-done.13
  15.1 102.8 %shard_map.158 = (f32[128,256]{1,0:T(8,128)S(1)}, f32[128,256]{1,0:T(8,128)S(1)}) custom-call(f32[128,256]{1,0:T(8,128)S(1)} %copy-done.5, f32[128,256]{1,0:T(8,128)S(1)} %copy-done.6, f32[128,256]{1,0:T(8,128)S(1)} %copy-done.7, f32[128,128]{1,0:T(8,128)S(1)} %copy-done.10, f32[1,256]{1,0:T(1,128)S(1)} %copy-done.12, s32[1,256]{1,0:T(1,128)S(1)} %copy-done.13, ...), custom_call_target="tpu_custom_call" | custom-call | tf_op jit(solution)/shard_map/pallas_call | solution.py:471
  117.9 0.7 copy.20
  118.6 0.7 copy.21
Async XLA Ops:
  1.3 1.4 %copy-start = (bf16[1536,512]{1,0:T(8,128)(2,1)S(1)}, bf16[1536,512]{1,0:T(8,128)(2,1)}, u32[]{:S(2)}) copy-start(bf16[1536,512]{1,0:T(8,128)(2,1)} %constant.17.clone.dt3_h) | copy-start | bytes 4718596
  2.7 1.4 %copy-start.1 = (bf16[1536,512]{1,0:T(8,128)(2,1)S(1)}, bf16[1536,512]{1,0:T(8,128)(2,1)}, u32[]{:S(2)}) copy-start(bf16[1536,512]{1,0:T(8,128)(2,1)} %constant.16.clone.d3_h) | copy-start | bytes 4718596
  4.1 1.2 %copy-start.2 = (f32[2,2,256,256]{3,2,1,0:T(8,128)S(1)}, f32[2,2,256,256]{3,2,1,0:T(8,128)}, u32[]{:S(2)}) copy-start(f32[2,2,256,256]{3,2,1,0:T(8,128)} %constant.18.clone.main_h) | copy-start | bytes 3145732
  5.3 1.1 copy-start.3
  6.5 1.1 copy-start.4
  7.6 0.9 copy-start.5
  8.5 0.9 copy-start.6
  9.4 0.9 copy-start.7
  10.3 0.9 copy-start.8
  11.2 0.9 copy-start.9
  12.1 0.8 copy-start.10
  13.0 0.8 copy-start.11
  13.7 0.7 copy-start.12
  14.4 0.7 copy-start.13

commit v2 on v1

v2 whole, which is shorter than its diff:
```python
import functools
import math

import jax
import jax.numpy as jnp
import ml_dtypes
import numpy as np
from jax import lax
from jax.experimental import pallas as pl
from jax.experimental.pallas import tpu as pltpu
from jax.sharding import PartitionSpec as P

SWEEPS = 4
ROUGH_STEP = 0.05
MESH = pl.DeviceIdType.MESH
F32 = jnp.float32
BF16 = jnp.bfloat16

N_ROLL, N_SIDE = 64, 8
ROWS, COLS = 128, 256
FFT_X, FFT_Y = 2 * N_ROLL * ROWS, 2 * N_SIDE * COLS
CLASSES = N_SIDE + 1


def split_np(x):
    x = x.astype(np.float32)
    hi = x.astype(ml_dtypes.bfloat16)
    lo = (x - hi.astype(np.float32)).astype(ml_dtypes.bfloat16)
    return hi, lo


def wide_np(x, axis):
    hi, lo = split_np(x)
    return np.concatenate([hi, hi, lo], axis=axis)


def turns(ints, length):
    return 2.0 * np.pi * (ints % length).astype(np.float64) / length


@functools.lru_cache(None)
def tables():
    a = np.arange(N_ROLL)
    ang = turns(a[:, None] * a[None, :], 2 * N_ROLL)
    sect = np.stack([np.cos(ang), -np.sin(ang)], axis=1)
    sect[0, 1] = np.where(a % 2 == 0, 1.0, -1.0)
    sect = np.einsum("uca,ij->uciaj", sect, np.eye(4)).reshape(8 * N_ROLL, 4 * N_ROLL)
    c = np.arange(COLS)
    ang = turns(c[:, None] * c[None, :], COLS)
    dcos, dsin = np.cos(ang), np.sin(ang)
    dft = np.block([[dcos, -dsin], [dsin, dcos]])
    v1 = np.arange(16)
    ang = turns(v1[:, None] * c[None, :], FFT_Y)
    twiddle = np.stack([np.cos(ang), np.sin(ang)]).astype(np.float32)
    q = np.arange(ROWS).reshape(N_SIDE, 16)
    t = np.arange(ROWS).reshape(32, 4)
    ang = turns(q[:, :, None, None] * t[None, None], ROWS)
    cb, sb = np.cos(ang), np.sin(ang)
    main = np.zeros((2, 2, 2, N_SIDE, 16, 32, 2, 4))
    main[1, 0, 0, :, :, :, 0], main[1, 0, 0, :, :, :, 1] = cb, sb
    main[1, 0, 1, :, :, :, 0], main[1, 0, 1, :, :, :, 1] = -sb, cb
    main[1, 1, 0, :, :, :, 0], main[1, 1, 0, :, :, :, 1] = -sb, cb
    main[1, 1, 1, :, :, :, 0], main[1, 1, 1, :, :, :, 1] = -cb, -sb
    even = np.where(q <= 64, q, q - 64)
    ang = turns(even[:, :, None, None] * t[None, None], ROWS)
    main[0, 0, 0, :, :, :, 0] = np.where((q <= 64)[:, :, None, None], np.cos(ang), np.sin(ang))
    odd = 64 + 128 * np.where(q < 64, q, q - 64)
    ang = turns(odd[:, :, None, None] * t[None, None], FFT_X)
    main[0, 0, 1, :, :, :, 1] = np.where((q < 64)[:, :, None, None], np.cos(ang), np.sin(ang))
    main = main.reshape(2, 2, 256, 256).astype(np.float32)
    cols_t = np.broadcast_to(t[:, None, :], (32, 2, 4)).reshape(256)
    ang = turns(a[:, None] * cols_t[None, :], FFT_X)
    slant = np.stack([np.cos(ang), np.sin(ang)], axis=1).astype(np.float32)
    return (
        wide_np(sect, 1),
        wide_np(sect.T, 1),
        wide_np(dft, 0),
        wide_np(dft.T, 0),
        main,
        slant,
        twiddle,
    )


def split(x):
    hi = x.astype(BF16)
    return hi, (x - hi.astype(F32)).astype(BF16)


def mm(a, b):
    return jnp.dot(a, b, preferred_element_type=F32)


def place(device):
    return lax.rem(device, 2) * 32 + lax.div(device, 2)


def combine(terms):
    total = None
    for coef, value in terms:
        if abs(coef) < 1e-12:
            continue
        if abs(coef - 1.0) < 1e-12:
            total = value if total is None else total + value
        elif abs(coef + 1.0) < 1e-12:
            total = -value if total is None else total - value
        else:
            total = coef * value if total is None else total + coef * value
    return total


def far(i, x, z, c):
    m, n = lax.div(i, 8), lax.div(lax.rem(i, 8), 2)
    dz = 4 + lax.div(m + 1, 2) * (1 - 2 * lax.rem(m, 2))
    dx = 2 + lax.div(n + 1, 2) * (1 - 2 * lax.rem(n, 2))
    return (
        lax.rem(x + dx, 4) * 16 + lax.rem(z + dz, 8) * 2 + lax.rem(c + 1 - lax.rem(i, 2), 2)
    )


def main_kernel(
    press_h, source_h, coupling_h, binv_h, lower_h, mask_h, rough_h, offset,
    w3_h, wt3_h, d3_h, dt3_h, main_h, slant_h, twid_h,
    newp_h, film_h,
    press, source, coupling, binv, lower, mask, rough, newp, film,
    w3, wt3, d3, dt3, maint, slant, twid,
    pack, halo, bhalo,
    cs, cr, outs0, outs, recv0, recv, gfull, carry_buf, gsel, bt, btt, bx, carry4, partner,
    b3, be3, loc4,
    kern, m3, mt3,
    p1s, p1r, qf, q3, p2s, p2r, x3, us, yb, zs, ob, ub, p5s, p5r, v3, p6s, p6r,
    const_sem, arg_sem, out_sem, halo_ss, halo_rs, ss, rs,
):
    me = lax.axis_index("roll")
    side = lax.axis_index("side")
    along_x, along_z, half = lax.div(me, 16), lax.rem(lax.div(me, 2), 8), lax.rem(me, 2)
    group = lax.div(me, 2)
    other = me + 1 - 2 * half
    barrier = pltpu.get_barrier_semaphore()

    def sig_roll(d, _):
        pl.semaphore_signal(
            barrier, inc=1, device_id={"roll": lax.rem(me + d, N_ROLL)}, device_id_type=MESH
        )
        return 0

    def sig_side(d, _):
        pl.semaphore_signal(
            barrier, inc=1, device_id={"side": lax.rem(side + d, N_SIDE)}, device_id_type=MESH
        )
        return 0

    lax.fori_loop(1, N_SIDE, sig_side, 0)
    lax.fori_loop(1, N_ROLL, sig_roll, 0)

    variant = jnp.minimum(me, 1)
    loads = [
        pltpu.make_async_copy(s, d, const_sem.at[i])
        for i, (s, d) in enumerate(
            [
                (w3_h, w3), (wt3_h, wt3), (d3_h, d3), (dt3_h, dt3),
                (main_h.at[variant], maint), (slant_h.at[me], slant), (twid_h, twid),
            ]
        )
    ]
    args = [
        pltpu.make_async_copy(s, d, arg_sem.at[i])
        for i, (s, d) in enumerate(
            [
                (press_h, press), (source_h, source), (coupling_h, coupling), (binv_h, binv),
                (lower_h, lower), (mask_h, mask), (rough_h, rough),
            ]
        )
    ]
    for load in args:
        load.start()
    for load in loads:
        load.start()

    def push(src, dst, phase, where):
        pltpu.make_async_remote_copy(
            src_ref=src, dst_ref=dst, send_sem=ss.at[phase], recv_sem=rs.at[phase],
            device_id=where, device_id_type=MESH,
        ).start()

    def send_roll(src_at, dst, phase):
        def body(i, _):
            to = far(i, along_x, along_z, half)
            push(src_at(to), dst, phase, {"roll": to})
            return 0

        lax.fori_loop(0, N_ROLL - 1, body, 0)

    def send_side(src_at, dst, phase):
        for d in (4, 3, 5, 2, 6, 1, 7):
            to = lax.rem(side + d, N_SIDE)
            push(src_at(to), dst, phase, {"side": to})

    def settle(src, dst, phase):
        pltpu.make_async_remote_copy(
            src_ref=src, dst_ref=dst, send_sem=ss.at[phase], recv_sem=rs.at[phase],
            device_id={"roll": other}, device_id_type=MESH,
        ).wait()

    rest = pl.ds(0, N_ROLL - 1)
    rest_side = pl.ds(0, N_SIDE - 1)

    lane_b = lax.broadcasted_iota(jnp.int32, (ROWS, 128), 1)
    for load in args[:6]:
        load.wait()
    for i, ref in enumerate((press, source, coupling)):
        pack[0, pl.ds(8 * i, 8), :] = ref[:, 0:128].T[0:8]
        pack[1, pl.ds(8 * i, 8), :] = ref[:, 128:256].T[120:128]
    for j in range(2):
        lanes = slice(128 * j, 128 * j + 128)
        pack[j, pl.ds(24, 8), :] = jnp.concatenate(
            [lower[:, lanes], mask[:, lanes].astype(F32), jnp.zeros((6, 128), F32)], axis=0
        )
    gain_m = binv[127:128, 0:1] * lower[...]
    first_row = binv[...].T[0:1]
    for j in range(2):
        lanes = slice(128 * j, 128 * j + 128)
        cs[j, 0:1, :] = gain_m[:, 0:128]
        cs[j, 1:2, :] = gain_m[:, 128:256]
        cs[j, 2:3, :] = lower[:, lanes]
        cs[j, 3:4, :] = mask[:, lanes].astype(F32)
        cs[j, 4:5, :] = first_row
    pl.semaphore_wait(barrier, N_ROLL + N_SIDE - 2)
    halo_copies = []
    for k in range(2):
        for j, d in ((0, N_SIDE - 1), (1, 1)):
            to = lax.rem(side + d, N_SIDE)
            s, dst = ((pack.at[j], halo.at[j]), (binv, bhalo.at[j]))[k]
            c = pltpu.make_async_remote_copy(
                src_ref=s, dst_ref=dst, send_sem=halo_ss.at[j, k], recv_sem=halo_rs.at[j, k],
                device_id={"side": to}, device_id_type=MESH,
            )
            c.start()
            halo_copies.append(c)
    send_roll(lambda to: cs.at[lax.rem(to, 2)], cr.at[me], 0)
    cr[me] = cs[half]
    bhi, blo = split(binv[...])
    b3[:, 0:128] = bhi
    b3[:, 128:256] = bhi
    b3[:, 256:384] = blo
    halo_copies[0].wait()
    halo_copies[1].wait()
    has_right = side < N_SIDE - 1
    has_left = side > 0
    is_right = lane_b < 64
    valid = jnp.logical_or(
        jnp.logical_and(is_right, has_right), jnp.logical_and(jnp.logical_not(is_right), has_left)
    )
    ext = []
    for i in range(3):
        tall = jnp.concatenate(
            [halo[0, pl.ds(8 * i, 8), :], jnp.zeros((112, 128), F32), halo[1, pl.ds(8 * i, 8), :]],
            axis=0,
        )
        ext.append(jnp.where(valid, tall.T, 0.0))
    row_right = is_right[0:1]
    row_valid = valid[0:1]
    lower_e = jnp.where(row_valid, jnp.where(row_right, halo[0, 24:25, :], halo[1, 24:25, :]), 0.0)
    mask_e = jnp.where(row_right, halo[0, 25:26, :], halo[1, 25:26, :]) > 0.5
    halo_copies[2].wait()
    halo_copies[3].wait()
    rhi, rlo = split(bhalo[0])
    lhi, llo = split(bhalo[1])
    for i, part in enumerate((rhi, lhi, rhi, lhi, rlo, llo)):
        be3[:, pl.ds(128 * i, 128)] = part
    first_e = jnp.where(is_right, bhalo[0, :, 0:1], bhalo[1, :, 0:1])
    first = binv[:, 0:1]
    lower_w = jnp.concatenate([lower[...], lower_e], axis=1)
    mask_w = jnp.concatenate([mask[...].astype(F32), mask_e.astype(F32)], axis=1) > 0.5
    first_w = jnp.concatenate([jnp.broadcast_to(first, (ROWS, COLS)), first_e], axis=1)
    source_w = jnp.concatenate([source[...], ext[1]], axis=1)
    coupling_w = jnp.concatenate([coupling[...], ext[2]], axis=1)
    field = jnp.concatenate([press[...], ext[0]], axis=1)
    outs0[3:4, :] = first_e[127:128] * lower_e

    for sweep in range(SWEEPS - 1):
        rhs = source_w + coupling_w * (pltpu.roll(field, 1, 1) + pltpu.roll(field, 383, 1))
        hi, lo = split(rhs[:, :256])
        stack = jnp.concatenate([hi, lo, hi], axis=0)
        he = rhs[:, 256:]
        hr, lr = split(jnp.where(is_right, he, 0.0))
        hl, ll = split(jnp.where(is_right, 0.0, he))
        stack_e = jnp.concatenate([hr, hl, lr, ll, hr, hl], axis=0)
        tail = mm(b3[112:128, :], stack)
        tail_e = mm(be3[112:128, :], stack_e)
        out = outs0 if sweep == 0 else outs.at[sweep - 1]
        for i in range(3):
            row = tail_e[15:16] if i == 2 else tail[15:16, 128 * i : 128 * i + 128]
            out[i : i + 1, :] = row
        into = recv0 if sweep == 0 else recv.at[sweep - 1]
        send_roll(lambda to: out, into.at[me], 1 + sweep)
        local = jnp.concatenate([mm(b3[...], stack), mm(be3[...], stack_e)], axis=1)
        if sweep == 0:
            i = lax.broadcasted_iota(jnp.int32, (16, COLS), 0)
            q = 16 * side + i
            lane = lax.broadcasted_iota(jnp.int32, (16, COLS), 1)
            reach = min(FFT_X, FFT_Y) / 16.0
            scale = 0.4 * reach / (float(FFT_X) * float(FFT_Y))
            for part in range(2):
                if part == 0:
                    u_first = 128 * jnp.where(q <= 64, q, q - 64)
                    single = jnp.logical_and(me == 0, jnp.logical_or(q == 0, q == 64))
                    weight = jnp.where(single, scale, 2.0 * scale)
                else:
                    u_first = 64 + 128 * jnp.where(q < 64, q, q - 64)
                    weight = jnp.full((16, COLS), 2.0 * scale, F32)
                u = jnp.where(me == 0, u_first, me + 128 * q)
                fu = jnp.minimum(u, FFT_X - u).astype(F32) / FFT_X
                fu2 = fu * fu
                for v1 in range(CLASSES):
                    v = v1 + 16 * lane
                    fv = jnp.minimum(v, FFT_Y - v).astype(F32) / FFT_Y
                    w = weight if v1 in (0, 8) else 2.0 * weight
                    kern[part, pl.ds(16 * v1, 16), :] = w / (
                        1.0 + reach * jnp.sqrt(fu2 + fv * fv)
                    )
            settle(cr.at[rest], cr.at[rest], 0)
            gfull[:, 0:2, :] = cr[:, 0:2, :]
        if sweep == 1:
            loads[4].wait()
            loads[5].wait()
            mrow = maint[0] * slant[0:1, :] + maint[1] * slant[1:2, :]
            hi, lo = split(mrow)
            m3[:, 0:256] = hi
            m3[:, 256:512] = hi
            m3[:, 512:768] = lo
            bt[...] = jnp.zeros_like(bt)
            for a in range(N_ROLL):
                bt[a : a + 1, :] = cr[a, 4:5, :]
                gsel[a] = jnp.where(half == 0, cr[a, 0:1, :], cr[a, 1:2, :])
        if sweep == 2:
            mrow = maint[0] * slant[0:1, :] + maint[1] * slant[1:2, :]
            hi, lo = split(mrow.T)
            mt3[:, 0:256] = hi
            mt3[:, 256:512] = hi
            mt3[:, 512:768] = lo
            btt[...] = bt[...].T.reshape(32, 4, 128)
            mine = btt[group]
            for a in range(N_ROLL):
                bx[a] = jnp.broadcast_to(mine[:, a : a + 1], (4, 128))
        settle(into.at[rest], into.at[rest], 1 + sweep)
        if sweep == 0:
            gfull[:, 2:3, :] = recv0[:, 3:4, :]

        def advance(k8, c):
            for j in range(8):
                k = 8 * k8 + j
                carry_buf[k] = c
                flow = recv0[k, 0:3] if sweep == 0 else recv[sweep - 1, k]
                c = flow + gfull[k] * c
            return c

        lax.fori_loop(0, N_ROLL // 8, advance, jnp.zeros((3, 128), F32))
        mine = carry_buf[me]
        carry = jnp.concatenate([mine[0:1], mine[1:2], mine[2:3]], axis=1)
        solved = local + first_w * (lower_w * carry)
        field = jnp.where(mask_w, jnp.maximum(solved, 0.0), solved)

    rhs = source_w + coupling_w * (pltpu.roll(field, 1, 1) + pltpu.roll(field, 383, 1))
    hi, lo = split(rhs[:, :256])
    local = mm(b3[...], jnp.concatenate([hi, lo, hi], axis=0))
    for h in range(2):
        tile = local[:, 128 * h : 128 * h + 128]
        p1s[pl.ds(32 * h, 32), 0:4, :] = tile.reshape(32, 4, 128)
        p1s[pl.ds(32 * h, 32), 4:5, :] = jnp.broadcast_to(tile[127:128].reshape(1, 1, 128), (32, 1, 128))
    send_roll(lambda to: p1s.at[place(to)], p1r.at[me], 4)
    p1r[me] = p1s[place(me)]
    loc4[...] = local
    loads[0].wait()
    settle(p1s.at[rest], p1r.at[rest], 4)

    def finish(k8, c):
        for j in range(8):
            k = 8 * k8 + j
            carry4[k] = c
            sol = p1r[k, 0:4, :] + bx[k] * (cr[k, 2:3, :] * c)
            qf[k] = jnp.where(cr[k, 3:4, :] > 0.5, jnp.maximum(sol, 0.0), sol)
            c = p1r[k, 4:5, :] + gsel[k] * c
        return c

    lax.fori_loop(0, N_ROLL // 8, finish, jnp.zeros((1, 128), F32))
    hi, lo = split(qf[...].reshape(256, 128))
    q3[0:256] = hi
    q3[256:512] = lo
    q3[512:768] = hi
    p2s[...] = mm(w3[...], q3[...]).reshape(64, 8, 128)

    send_roll(lambda to: p2s.at[to], p2r.at[place(me)], 5)
    push(carry4.at[other], partner, 6, {"roll": other})
    p2r[place(me)] = p2s[me]
    settle(carry4.at[0], partner, 6)
    for h in range(2):
        lanes = slice(128 * h, 128 * h + 128)
        carry = jnp.where(half == h, carry4[me], partner[...])
        sol = loc4[:, lanes] + binv[:, 0:1] * (lower[:, lanes] * carry)
        newp[:, lanes] = jnp.where(mask[:, lanes] == 1, jnp.maximum(sol, 0.0), sol)
    save_p = pltpu.make_async_copy(newp, newp_h, out_sem.at[0])
    save_p.start()
    settle(p2s.at[rest], p2r.at[rest], 5)
    for h in range(2):
        hi, lo = split(p2r[pl.ds(32 * h, 32)].reshape(256, 128))
        lanes = slice(128 * h, 128 * h + 128)
        x3[0:256, lanes] = hi
        x3[256:512, lanes] = lo
        x3[512:768, lanes] = hi

    for part in range(2):
        us[part] = mm(m3[128 * part : 128 * part + 128, :], x3[...]).reshape(8, 16, 256)
        send_side(lambda to: us.at[part, to], yb.at[part, side], 7 + part)
        yb[part, side] = us[part, side]
    loads[2].wait()
    loads[3].wait()
    loads[6].wait()

    cosines = [[math.cos(math.pi * s * v / 8.0) for v in range(9)] for s in range(8)]
    sines = [[math.sin(math.pi * s * v / 8.0) for v in range(9)] for s in range(8)]

    def put(v1, lanes, re, im):
        at = 16 * v1
        for which, value in ((0, re), (256, im)):
            hi, lo = split(value)
            zs[pl.ds(at, 16), pl.ds(which + lanes, 128)] = hi
            zs[pl.ds(at, 16), pl.ds(512 + which + lanes, 128)] = lo
            zs[pl.ds(at, 16), pl.ds(1024 + which + lanes, 128)] = hi

    for part in range(2):
        settle(us.at[part, rest_side], yb.at[part, rest_side], 7 + part)
        for lanes in (0, 128):
            x = [yb[part, s, :, pl.ds(lanes, 128)] for s in range(8)]
            for v in range(5):
                er = combine([(cosines[s][v], x[s]) for s in (0, 2, 4, 6)])
                orr = combine([(cosines[s][v], x[s]) for s in (1, 3, 5, 7)])
                ei = combine([(-sines[s][v], x[s]) for s in (0, 2, 4, 6)])
                oi = combine([(-sines[s][v], x[s]) for s in (1, 3, 5, 7)])
                zero = jnp.zeros((16, 128), F32)
                ei = zero if ei is None else ei
                oi = zero if oi is None else oi
                orr = zero if orr is None else orr
                todo = [(v, er + orr, ei + oi)]
                if v < 4:
                    todo.append((8 - v, er - orr, oi - ei))
                for v1, yr, yi in todo:
                    c = twid[0, v1 : v1 + 1, lanes : lanes + 128]
                    s = twid[1, v1 : v1 + 1, lanes : lanes + 128]
                    put(v1, lanes, yr * c + yi * s, yi * c - yr * s)
        spec = mm(zs[...], d3[...])
        for v1 in range(CLASSES):
            at = 16 * v1
            for lanes in (0, 128):
                k = kern[part, pl.ds(at, 16), pl.ds(lanes, 128)]
                put(
                    v1, lanes,
                    spec[at : at + 16, lanes : lanes + 128] * k,
                    spec[at : at + 16, 256 + lanes : 384 + lanes] * k,
                )
        back = mm(zs[...], dt3[...])
        for lanes in (0, 128):
            yr, yi = [], []
            for v1 in range(CLASSES):
                at = 16 * v1
                zr = back[at : at + 16, lanes : lanes + 128]
                zi = back[at : at + 16, 256 + lanes : 384 + lanes]
                c = twid[0, v1 : v1 + 1, lanes : lanes + 128]
                s = twid[1, v1 : v1 + 1, lanes : lanes + 128]
                yr.append(zr * c - zi * s)
                yi.append(zr * s + zi * c)
            plus_r = [yr[v] + yr[8 - v] for v in range(4)] + [yr[4]]
            plus_i = [yi[v] + yi[8 - v] for v in range(4)] + [yi[4]]
            less_r = [yr[v] - yr[8 - v] for v in range(4)] + [yr[4]]
            less_i = [yi[v] - yi[8 - v] for v in range(4)] + [yi[4]]
            h = lanes // 128
            for s in range(8):
                re, im = (plus_r, less_i) if s % 2 == 0 else (less_r, plus_i)
                ob[h, part, s] = combine(
                    [(cosines[s][v], re[v]) for v in range(5)]
                    + [(-sines[s][v], im[v]) for v in range(5)]
                )
            send_side(lambda to: ob.at[h, part, to], ub.at[h, part, side], 9 + 2 * h + part)
            ub[h, part, side] = ob[h, part, side]

    for h in range(2):
        for part in range(2):
            settle(ob.at[h, part, rest_side], ub.at[h, part, rest_side], 9 + 2 * h + part)
        hi, lo = split(ub[h].reshape(256, 128))
        v3[0:256] = hi
        v3[256:512] = lo
        v3[512:768] = hi
        p5s[pl.ds(32 * h, 32)] = mm(mt3[...], v3[0:768]).reshape(32, 8, 128)

        def body(i, _):
            to = far(2 * i + 1, along_x, along_z, h)
            push(p5s.at[place(to)], p5r.at[me], 13, {"roll": to})
            return 0

        lax.fori_loop(0, 31, body, 0)

        @pl.when(half != h)
        def _():
            push(p5s.at[place(other)], p5r.at[me], 13, {"roll": other})

    p5r[me] = p5s[place(me)]
    loads[1].wait()
    settle(p5s.at[rest], p5r.at[rest], 13)
    hi, lo = split(p5r[...].reshape(512, 128))
    v3[0:512] = hi
    v3[512:1024] = lo
    v3[1024:1536] = hi
    p6s[...] = mm(wt3[...], v3[...]).reshape(64, 4, 128)

    send_roll(lambda to: p6s.at[to], p6r.at[place(me)], 14)
    p6r[place(me)] = p6s[me]
    row_pos = (me * ROWS + lax.broadcasted_iota(jnp.int32, (ROWS, COLS), 0)).astype(F32)
    col_pos = (side * COLS + lax.broadcasted_iota(jnp.int32, (ROWS, COLS), 1)).astype(F32)
    across = 4.0 * (row_pos + 0.5) / (ROWS * N_ROLL) - 2.5
    transverse = 4.0 * (col_pos + 0.5) / (COLS * N_SIDE) - 2.0
    ground = offset[0] + 0.5 * across * across + 0.5 * transverse * transverse
    args[6].wait()
    ripple = ROUGH_STEP * rough[...].astype(F32)
    settle(p6s.at[rest], p6r.at[rest], 14)
    for h in range(2):
        lanes = slice(128 * h, 128 * h + 128)
        bend = p6r[pl.ds(32 * h, 32)].reshape(128, 128)
        film[:, lanes] = ground[:, lanes] + bend - ripple[:, lanes]
    save_f = pltpu.make_async_copy(film, film_h, out_sem.at[1])
    save_f.start()
    save_p.wait()
    save_f.wait()


def per_device(pressure, source, coupling, binv, lower, mask, rough, offset):
    consts = [jnp.asarray(t) for t in tables()]
    hbm = pl.BlockSpec(memory_space=pl.ANY)
    f = lambda *shape: pltpu.VMEM(shape, F32)
    b = lambda *shape: pltpu.VMEM(shape, BF16)
    i32 = lambda *shape: pltpu.VMEM(shape, jnp.int32)
    scratch = [
        f(128, 256), f(128, 256), f(128, 256), f(128, 128), f(1, 256), i32(1, 256), i32(128, 256),
        f(128, 256), f(128, 256),
        b(512, 768), b(256, 1536), b(1536, 512), b(1536, 512),
        f(2, 256, 256), f(2, 256), f(2, 16, 256),
        f(2, 32, 128), f(2, 32, 128), f(2, 128, 128),
        f(2, 5, 128), f(64, 5, 128), f(4, 128), f(2, 3, 128), f(64, 4, 128), f(2, 64, 3, 128),
        f(64, 3, 128), f(64, 3, 128), f(64, 1, 128), f(128, 128), f(32, 4, 128), f(64, 4, 128),
        f(64, 1, 128), f(1, 128),
        b(128, 384), b(128, 768), f(128, 256),
        f(2, 144, 256), b(256, 768), b(256, 768),
        f(64, 5, 128), f(64, 5, 128), f(64, 4, 128), b(768, 128), f(64, 8, 128), f(64, 8, 128),
        b(768, 256), f(2, 8, 16, 256), f(2, 8, 16, 256), b(144, 1536), f(2, 2, 8, 16, 128),
        f(2, 2, 8, 16, 128), f(64, 8, 128), f(64, 8, 128), b(1536, 128), f(64, 4, 128),
        f(64, 4, 128),
        pltpu.SemaphoreType.DMA((7,)), pltpu.SemaphoreType.DMA((7,)), pltpu.SemaphoreType.DMA((2,)),
        pltpu.SemaphoreType.DMA((2, 2)), pltpu.SemaphoreType.DMA((2, 2)),
        pltpu.SemaphoreType.DMA((15,)), pltpu.SemaphoreType.DMA((15,)),
    ]
    out = jax.ShapeDtypeStruct((ROWS, COLS), F32)
    return pl.pallas_call(
        main_kernel,
        out_shape=(out, out),
        in_specs=[hbm] * 7 + [pl.BlockSpec(memory_space=pltpu.SMEM)] + [hbm] * 7,
        out_specs=(hbm, hbm),
        scratch_shapes=scratch,
        compiler_params=pltpu.CompilerParams(
            collective_id=0, has_side_effects=True, vmem_limit_bytes=56 * 1024 * 1024
        ),
    )(pressure, source, coupling, binv, lower, mask, rough, offset, *consts)


def solution(mesh):
    spec = P("roll", "side")
    return jax.shard_map(
        per_device,
        mesh=mesh,
        in_specs=(spec,) * 7 + (P(),),
        out_specs=(spec, spec),
        check_vma=False,
    )
```

time: 121 us -> 94.5 us (0.78); the launches traced: 119 us -> 94.3 us
  Pallas kernels: 103 us -> 89.9 us
  local copies, waits for them, and re-layouts: 15.1 us -> 3.14 us
    pallas_call x1, Pallas kernels: 103 us -> 89.9 us  [per_device(): pl.pallas_call(main_kernel, out_shape=(out, out), in_specs=[hbm] * 7 + [p...]
    unnamed x30 -> x2, local copies, waits for them, and re-layouts: 15.1 us -> 3.14 us
where the time goes in v2:
time: 94.5 us; the launch traced here: 94.3 us
  Pallas kernels  89.9 us (95%)
  local copies, waits for them, and re-layouts  3.14 us (3%)
  between operations  1.29 us (1%)
    pallas_call x1, Pallas kernels, per_device(): pl.pallas_call(main_kernel, out_shape=(out, out), in_specs=[hbm] * 7 + [p...  89.9 us
    unnamed x2, local copies, waits for them, and re-layouts  3.14 us

profile of v2, /device:TPU:1, one launch (start us, length us, event | category | flops | bytes accessed | tf_op | source)
XLA Modules:
  0.0 94.3 jit_solution(10250769820923087543)
XLA Ops:
  1.3 89.9 %shard_map.158 = (f32[128,256]{1,0:T(8,128)}, f32[128,256]{1,0:T(8,128)}) custom-call(f32[128,256]{1,0:T(8,128)} %press_h.1, f32[128,256]{1,0:T(8,128)} %source_h.1, f32[128,256]{1,0:T(8,128)} %coupling_h.1, f32[128,128]{1,0:T(8,128)} %binv_h.1, f32[1,256]{1,0:T(1,128)} %lower_h.1, s32[1,256]{1,0:T(1,128)} %mask_h.1, s32[128,256]{1,0:T(8,128)} %rough_h.1, ...), custom_call_target="tpu_custom_call" | custom-call | tf_op jit(solution)/shard_map/pallas_call | solution.py:561
  91.2 1.6 %copy.20 = f32[128,256]{1,0:T(8,128)} copy(f32[128,256]{1,0:T(8,128)} %get-tuple-element.4) | data formatting | bytes 262144
  92.7 1.6 %copy.21 = f32[128,256]{1,0:T(8,128)} copy(f32[128,256]{1,0:T(8,128)} %get-tuple-element.5) | data formatting | bytes 262144

commit v3 on v2

--- a/solution.py
+++ b/solution.py
@@ -121,15 +121,15 @@
 def main_kernel(
     press_h, source_h, coupling_h, binv_h, lower_h, mask_h, rough_h, offset,
     w3_h, wt3_h, d3_h, dt3_h, main_h, slant_h, twid_h,
-    newp_h, film_h,
-    press, source, coupling, binv, lower, mask, rough, newp, film,
+    newp, film,
+    press, source, coupling, binv, lower, mask, rough,
     w3, wt3, d3, dt3, maint, slant, twid,
     pack, halo, bhalo,
-    cs, cr, outs0, outs, recv0, recv, gfull, carry_buf, gsel, bt, btt, bx, carry4, partner,
+    cs, cr, outs0, outs, recv0, recv, gfull, gpre, gall, cgroup, carry_buf, gsel, gsel_pre, gsel_all, bt, btt, bx, carry4, partner,
     b3, be3, loc4,
     kern, m3, mt3,
     p1s, p1r, qf, q3, p2s, p2r, x3, us, yb, zs, ob, ub, p5s, p5r, v3, p6s, p6r,
-    const_sem, arg_sem, out_sem, halo_ss, halo_rs, ss, rs,
+    const_sem, arg_sem, known, halo_ss, halo_rs, ss, rs,
 ):
     me = lax.axis_index("roll")
     side = lax.axis_index("side")
@@ -138,20 +138,20 @@
     other = me + 1 - 2 * half
     barrier = pltpu.get_barrier_semaphore()
 
-    def sig_roll(d, _):
-        pl.semaphore_signal(
-            barrier, inc=1, device_id={"roll": lax.rem(me + d, N_ROLL)}, device_id_type=MESH
-        )
-        return 0
-
-    def sig_side(d, _):
-        pl.semaphore_signal(
-            barrier, inc=1, device_id={"side": lax.rem(side + d, N_SIDE)}, device_id_type=MESH
-        )
-        return 0
-
-    lax.fori_loop(1, N_SIDE, sig_side, 0)
-    lax.fori_loop(1, N_ROLL, sig_roll, 0)
+    def greet(sem, where):
+        pl.semaphore_signal(sem, inc=1, device_id=where, device_id_type=MESH)
+
+    def plane(i):
+        n = lax.div(i, 2)
+        dx = 2 + lax.div(n + 1, 2) * (1 - 2 * lax.rem(n, 2))
+        core = lax.rem(half + 1 - lax.rem(i, 2), 2)
+        return lax.rem(along_x + dx, 4) * 16 + along_z * 2 + core
+
+    for d in (4, 3, 5, 2, 6, 1, 7):
+        greet(barrier, {"roll": along_x * 16 + lax.rem(along_z + d, 8) * 2 + half})
+        greet(barrier, {"side": lax.rem(side + d, N_SIDE)})
+    for i in range(7):
+        greet(barrier, {"roll": plane(i)})
 
     variant = jnp.minimum(me, 1)
     loads = [
@@ -225,7 +225,7 @@
         cs[j, 2:3, :] = lower[:, lanes]
         cs[j, 3:4, :] = mask[:, lanes].astype(F32)
         cs[j, 4:5, :] = first_row
-    pl.semaphore_wait(barrier, N_ROLL + N_SIDE - 2)
+    pl.semaphore_wait(barrier, 21)
     halo_copies = []
     for k in range(2):
         for j, d in ((0, N_SIDE - 1), (1, 1)):
@@ -237,12 +237,15 @@
             )
             c.start()
             halo_copies.append(c)
-    send_roll(lambda to: cs.at[lax.rem(to, 2)], cr.at[me], 0)
+    for i in range(7):
+        greet(known, {"roll": plane(i)})
     cr[me] = cs[half]
     bhi, blo = split(binv[...])
     b3[:, 0:128] = bhi
     b3[:, 128:256] = bhi
     b3[:, 256:384] = blo
+    pl.semaphore_wait(known, 7)
+    send_roll(lambda to: cs.at[lax.rem(to, 2)], cr.at[me], 0)
     halo_copies[0].wait()
     halo_copies[1].wait()
     has_right = side < N_SIDE - 1
@@ -262,21 +265,12 @@
     row_valid = valid[0:1]
     lower_e = jnp.where(row_valid, jnp.where(row_right, halo[0, 24:25, :], halo[1, 24:25, :]), 0.0)
     mask_e = jnp.where(row_right, halo[0, 25:26, :], halo[1, 25:26, :]) > 0.5
-    halo_copies[2].wait()
-    halo_copies[3].wait()
-    rhi, rlo = split(bhalo[0])
-    lhi, llo = split(bhalo[1])
-    for i, part in enumerate((rhi, lhi, rhi, lhi, rlo, llo)):
-        be3[:, pl.ds(128 * i, 128)] = part
-    first_e = jnp.where(is_right, bhalo[0, :, 0:1], bhalo[1, :, 0:1])
     first = binv[:, 0:1]
     lower_w = jnp.concatenate([lower[...], lower_e], axis=1)
     mask_w = jnp.concatenate([mask[...].astype(F32), mask_e.astype(F32)], axis=1) > 0.5
-    first_w = jnp.concatenate([jnp.broadcast_to(first, (ROWS, COLS)), first_e], axis=1)
     source_w = jnp.concatenate([source[...], ext[1]], axis=1)
     coupling_w = jnp.concatenate([coupling[...], ext[2]], axis=1)
     field = jnp.concatenate([press[...], ext[0]], axis=1)
-    outs0[3:4, :] = first_e[127:128] * lower_e
 
     for sweep in range(SWEEPS - 1):
         rhs = source_w + coupling_w * (pltpu.roll(field, 1, 1) + pltpu.roll(field, 383, 1))
@@ -287,6 +281,16 @@
         hl, ll = split(jnp.where(is_right, 0.0, he))
         stack_e = jnp.concatenate([hr, hl, lr, ll, hr, hl], axis=0)
         tail = mm(b3[112:128, :], stack)
+        if sweep == 0:
+            halo_copies[2].wait()
+            halo_copies[3].wait()
+            rhi, rlo = split(bhalo[0])
+            lhi, llo = split(bhalo[1])
+            for i, part in enumerate((rhi, lhi, rhi, lhi, rlo, llo)):
+                be3[:, pl.ds(128 * i, 128)] = part
+            first_e = jnp.where(is_right, bhalo[0, :, 0:1], bhalo[1, :, 0:1])
+            first_w = jnp.concatenate([jnp.broadcast_to(first, (ROWS, COLS)), first_e], axis=1)
+            outs0[3:4, :] = first_e[127:128] * lower_e
         tail_e = mm(be3[112:128, :], stack_e)
         out = outs0 if sweep == 0 else outs.at[sweep - 1]
         for i in range(3):
@@ -332,7 +336,12 @@
             bt[...] = jnp.zeros_like(bt)
             for a in range(N_ROLL):
                 bt[a : a + 1, :] = cr[a, 4:5, :]
-                gsel[a] = jnp.where(half == 0, cr[a, 0:1, :], cr[a, 1:2, :])
+                gain = jnp.where(half == 0, cr[a, 0:1, :], cr[a, 1:2, :])
+                gsel[a] = gain
+                gsel_pre[a] = jnp.ones((1, 128), F32) if a % 8 == 0 else product
+                product = gain if a % 8 == 0 else product * gain
+                if a % 8 == 7:
+                    gsel_all[a // 8] = product
         if sweep == 2:
             mrow = maint[0] * slant[0:1, :] + maint[1] * slant[1:2, :]
             hi, lo = split(mrow.T)
@@ -347,16 +356,26 @@
         if sweep == 0:
             gfull[:, 2:3, :] = recv0[:, 3:4, :]
 
-        def advance(k8, c):
+        totals = []
+        for g in range(8):
+            c = flow = None
             for j in range(8):
-                k = 8 * k8 + j
-                carry_buf[k] = c
+                k = 8 * g + j
                 flow = recv0[k, 0:3] if sweep == 0 else recv[sweep - 1, k]
-                c = flow + gfull[k] * c
-            return c
-
-        lax.fori_loop(0, N_ROLL // 8, advance, jnp.zeros((3, 128), F32))
-        mine = carry_buf[me]
+                gain = gfull[k]
+                carry_buf[k] = jnp.zeros((3, 128), F32) if c is None else c
+                c = flow if c is None else flow + gain * c
+                if sweep == 0:
+                    gpre[k] = jnp.ones((3, 128), F32) if j == 0 else product
+                    product = gain if j == 0 else product * gain
+            if sweep == 0:
+                gall[g] = product
+            totals.append(c)
+        c = jnp.zeros((3, 128), F32)
+        for g in range(8):
+            cgroup[g] = c
+            c = totals[g] + gall[g] * c
+        mine = carry_buf[me] + gpre[me] * cgroup[lax.div(me, 8)]
         carry = jnp.concatenate([mine[0:1], mine[1:2], mine[2:3]], axis=1)
         solved = local + first_w * (lower_w * carry)
         field = jnp.where(mask_w, jnp.maximum(solved, 0.0), solved)
@@ -374,16 +393,24 @@
     loads[0].wait()
     settle(p1s.at[rest], p1r.at[rest], 4)
 
-    def finish(k8, c):
+    inner, totals = [], []
+    for g in range(8):
+        c = None
         for j in range(8):
-            k = 8 * k8 + j
-            carry4[k] = c
-            sol = p1r[k, 0:4, :] + bx[k] * (cr[k, 2:3, :] * c)
+            k = 8 * g + j
+            inner.append(c)
+            flow = p1r[k, 4:5, :]
+            c = flow if c is None else flow + gsel[k] * c
+        totals.append(c)
+    c = jnp.zeros((1, 128), F32)
+    for g in range(8):
+        for j in range(8):
+            k = 8 * g + j
+            ck = c if j == 0 else inner[k] + gsel_pre[k] * c
+            carry4[k] = ck
+            sol = p1r[k, 0:4, :] + bx[k] * (cr[k, 2:3, :] * ck)
             qf[k] = jnp.where(cr[k, 3:4, :] > 0.5, jnp.maximum(sol, 0.0), sol)
-            c = p1r[k, 4:5, :] + gsel[k] * c
-        return c
-
-    lax.fori_loop(0, N_ROLL // 8, finish, jnp.zeros((1, 128), F32))
+        c = totals[g] + gsel_all[g] * c
     hi, lo = split(qf[...].reshape(256, 128))
     q3[0:256] = hi
     q3[256:512] = lo
@@ -399,8 +426,6 @@
         carry = jnp.where(half == h, carry4[me], partner[...])
         sol = loc4[:, lanes] + binv[:, 0:1] * (lower[:, lanes] * carry)
         newp[:, lanes] = jnp.where(mask[:, lanes] == 1, jnp.maximum(sol, 0.0), sol)
-    save_p = pltpu.make_async_copy(newp, newp_h, out_sem.at[0])
-    save_p.start()
     settle(p2s.at[rest], p2r.at[rest], 5)
     for h in range(2):
         hi, lo = split(p2r[pl.ds(32 * h, 32)].reshape(256, 128))
@@ -526,10 +551,6 @@
         lanes = slice(128 * h, 128 * h + 128)
         bend = p6r[pl.ds(32 * h, 32)].reshape(128, 128)
         film[:, lanes] = ground[:, lanes] + bend - ripple[:, lanes]
-    save_f = pltpu.make_async_copy(film, film_h, out_sem.at[1])
-    save_f.start()
-    save_p.wait()
-    save_f.wait()
 
 
 def per_device(pressure, source, coupling, binv, lower, mask, rough, offset):
@@ -540,12 +561,12 @@
     i32 = lambda *shape: pltpu.VMEM(shape, jnp.int32)
     scratch = [
         f(128, 256), f(128, 256), f(128, 256), f(128, 128), f(1, 256), i32(1, 256), i32(128, 256),
-        f(128, 256), f(128, 256),
         b(512, 768), b(256, 1536), b(1536, 512), b(1536, 512),
         f(2, 256, 256), f(2, 256), f(2, 16, 256),
         f(2, 32, 128), f(2, 32, 128), f(2, 128, 128),
         f(2, 5, 128), f(64, 5, 128), f(4, 128), f(2, 3, 128), f(64, 4, 128), f(2, 64, 3, 128),
-        f(64, 3, 128), f(64, 3, 128), f(64, 1, 128), f(128, 128), f(32, 4, 128), f(64, 4, 128),
+        f(64, 3, 128), f(64, 3, 128), f(8, 3, 128), f(8, 3, 128), f(64, 3, 128), f(64, 1, 128),
+        f(64, 1, 128), f(8, 1, 128), f(128, 128), f(32, 4, 128), f(64, 4, 128),
         f(64, 1, 128), f(1, 128),
         b(128, 384), b(128, 768), f(128, 256),
         f(2, 144, 256), b(256, 768), b(256, 768),
@@ -553,16 +574,16 @@
         b(768, 256), f(2, 8, 16, 256), f(2, 8, 16, 256), b(144, 1536), f(2, 2, 8, 16, 128),
         f(2, 2, 8, 16, 128), f(64, 8, 128), f(64, 8, 128), b(1536, 128), f(64, 4, 128),
         f(64, 4, 128),
-        pltpu.SemaphoreType.DMA((7,)), pltpu.SemaphoreType.DMA((7,)), pltpu.SemaphoreType.DMA((2,)),
+        pltpu.SemaphoreType.DMA((7,)), pltpu.SemaphoreType.DMA((7,)), pltpu.SemaphoreType.REGULAR,
         pltpu.SemaphoreType.DMA((2, 2)), pltpu.SemaphoreType.DMA((2, 2)),
         pltpu.SemaphoreType.DMA((15,)), pltpu.SemaphoreType.DMA((15,)),
     ]
-    out = jax.ShapeDtypeStruct((ROWS, COLS), F32)
+    out = pltpu.VMEM((ROWS, COLS), F32)
     return pl.pallas_call(
         main_kernel,
         out_shape=(out, out),
         in_specs=[hbm] * 7 + [pl.BlockSpec(memory_space=pltpu.SMEM)] + [hbm] * 7,
-        out_specs=(hbm, hbm),
+        out_specs=(pl.BlockSpec(memory_space=pltpu.VMEM),) * 2,
         scratch_shapes=scratch,
         compiler_params=pltpu.CompilerParams(
             collective_id=0, has_side_effects=True, vmem_limit_bytes=56 * 1024 * 1024

time: 94.5 us -> 90.9 us (0.962)
  local copies, waits for them, and re-layouts: 3.14 us -> 1.31 us
  Pallas kernels: 89.9 us -> 88.2 us
    unnamed x2, local copies, waits for them, and re-layouts: 3.14 us -> 1.31 us
    pallas_call x1, Pallas kernels: 89.9 us -> 88.2 us  [per_device(): pl.pallas_call(main_kernel, out_shape=(out, out), in_specs=[hbm] * 7 + [p...]
where the time goes in v3:
time: 90.9 us; the launch traced here: 90.8 us
  Pallas kernels  88.2 us (97%)
  local copies, waits for them, and re-layouts  1.31 us (1%)
  between operations  1.29 us (1%)
    pallas_call x1, Pallas kernels, per_device(): pl.pallas_call(main_kernel, out_shape=(out, out), in_specs=[hbm] * 7 + [p...  88.2 us

profile of v3, /device:TPU:1, one launch (start us, length us, event | category | flops | bytes accessed | tf_op | source)
XLA Modules:
  0.0 90.8 jit_solution(16123684409817133718)
XLA Ops:
  1.3 88.2 %shard_map.158 = (f32[128,256]{1,0:T(8,128)S(1)}, f32[128,256]{1,0:T(8,128)S(1)}) custom-call(f32[128,256]{1,0:T(8,128)} %press_h.1, f32[128,256]{1,0:T(8,128)} %source_h.1, f32[128,256]{1,0:T(8,128)} %coupling_h.1, f32[128,128]{1,0:T(8,128)} %binv_h.1, f32[1,256]{1,0:T(1,128)} %lower_h.1, s32[1,256]{1,0:T(1,128)} %mask_h.1, s32[128,256]{1,0:T(8,128)} %rough_h.1, ...), custom_call_target="tpu_custom_call" | custom-call | tf_op jit(solution)/shard_map/pallas_call | solution.py:582
  89.5 0.7 copy.19
  90.1 0.7 copy.20

commit v4 on v3

--- a/solution.py
+++ b/solution.py
@@ -189,7 +189,7 @@
             push(src_at(to), dst, phase, {"roll": to})
             return 0
 
-        lax.fori_loop(0, N_ROLL - 1, body, 0)
+        lax.fori_loop(0, N_ROLL - 1, body, 0, unroll=63)
 
     def send_side(src_at, dst, phase):
         for d in (4, 3, 5, 2, 6, 1, 7):

time: 90.9 us -> 89.5 us (0.985)
  Pallas kernels: 88.2 us -> 86.8 us
    pallas_call x1, Pallas kernels: 88.2 us -> 86.8 us  [per_device(): pl.pallas_call(main_kernel, out_shape=(out, out), in_specs=[hbm] * 7 + [p...]
where the time goes in v4:
time: 89.5 us; the launch traced here: 89.4 us
  Pallas kernels  86.8 us (97%)
  local copies, waits for them, and re-layouts  1.31 us (1%)
  between operations  1.29 us (1%)
    pallas_call x1, Pallas kernels, per_device(): pl.pallas_call(main_kernel, out_shape=(out, out), in_specs=[hbm] * 7 + [p...  86.8 us

profile of v4, /device:TPU:1, one launch (start us, length us, event | category | flops | bytes accessed | tf_op | source)
XLA Modules:
  0.0 89.4 jit_solution(13657211844778096482)
XLA Ops:
  1.3 86.8 %shard_map.158 = (f32[128,256]{1,0:T(8,128)S(1)}, f32[128,256]{1,0:T(8,128)S(1)}) custom-call(f32[128,256]{1,0:T(8,128)} %press_h.1, f32[128,256]{1,0:T(8,128)} %source_h.1, f32[128,256]{1,0:T(8,128)} %coupling_h.1, f32[128,128]{1,0:T(8,128)} %binv_h.1, f32[1,256]{1,0:T(1,128)} %lower_h.1, s32[1,256]{1,0:T(1,128)} %mask_h.1, s32[128,256]{1,0:T(8,128)} %rough_h.1, ...), custom_call_target="tpu_custom_call" | custom-call | tf_op jit(solution)/shard_map/pallas_call | solution.py:582
  88.1 0.7 copy.19
  88.7 0.7 copy.20
